TPU v7x, 256 devices: a whole 4x4x8 slice. The times are simulated.
256 devices in a mesh: expert: 16 (over x, y_hi, core), tensor: 8 (over z), dp: 2 (over y_lo).
Axes of the slice: x: 4, y: 4 (y_hi: 2, y_lo: 2; y = y_hi * 2 + y_lo), z: 8, core: 2. Of those that a mesh axis runs over, the one named last changes fastest.
Arguments:
- tokens: bfloat16 [8192, 3072], P(('expert', 'dp'), 'tensor'), may hold values from -6 to 6
- out_grad: bfloat16 [8192, 3072], P(('expert', 'dp'), 'tensor'), may hold values from -6 to 6
- gate_weight: bfloat16 [5376, 3072], P('expert', 'tensor'), may hold values from -0.109375 to 0.109375
- up_weight: bfloat16 [5376, 3072], P('expert', 'tensor'), may hold values from -0.109375 to 0.109375
- down_weight: bfloat16 [5376, 3072], P('expert', 'tensor'), may hold values from -0.078125 to 0.078125
- route_count: int32 [32], P(('expert', 'dp')), may hold values from 24 to 96, as said below
- route_index: int32 [3072], P(('expert', 'dp')), may hold values from 0 to 255, as said below
- route_gate: float32 [3072], P(('expert', 'dp')), may hold values from 0.1 to 1
Outputs:
- mixed: bfloat16 [8192, 3072], P(('expert', 'dp'), 'tensor')
- input_grad: bfloat16 [8192, 3072], P(('expert', 'dp'), 'tensor')
- grad_gate: float32 [5376, 3072], P('expert', ('tensor', 'dp'))
- grad_up: float32 [5376, 3072], P('expert', ('tensor', 'dp'))
- grad_down: float32 [5376, 3072], P('expert', ('tensor', 'dp'))
Inputs may be any that keep to these rules, and one draw needn't show every extreme that they name: `route_count`: one shard's count is exactly 96 and another's exactly 24. `route_index`: within one shard's 96 slots the token indices are distinct.
All inputs are finite; a program needn't handle non-finite values.
Results may differ from a plain program's by a relative error of at most 0.035.
Values may be sent and summed in bfloat16 or wider, within the bound.
No kernel may reach another device: no remote copies, remote signals or barrier semaphores. Data moves between devices by JAX's collectives and lax.ppermute only.
A program may use at most 64 MiB of HBM per device.

v0:
```python
import functools

import jax
import jax.numpy as jnp
from jax import lax
from jax.experimental import pallas as pl
from jax.experimental.pallas import tpu as pltpu
from jax.sharding import Mesh
from jax.sharding import PartitionSpec as P

BF16 = jnp.bfloat16
F32 = jnp.float32
XS, YS, CORES, RING = 4, 2, 2, 8
CHIPS = XS * YS
FIRST, LAST = 640, 768
VMEM_LIMIT = 40 * 1024 * 1024
FETCH_LIMIT = 60 * 1024 * 1024
WHOLE = pl.BlockSpec(memory_space=pltpu.VMEM)
SCALARS = pl.BlockSpec(memory_space=pltpu.SMEM)


def dot(left, right, left_dim, right_dim):
    return lax.dot_general(
        left, right, (((left_dim,), (right_dim,)), ((), ())), preferred_element_type=F32
    )


def core_swap(x):
    return lax.ppermute(x, "core", [(0, 1), (1, 0)])


def among_chips(x):
    return lax.all_to_all(x, ("x", "y"), 0, 0, tiled=True)


def along_x(x, by):
    return lax.ppermute(x, "x", [(i, (i + by) % XS) for i in range(XS)])


def ring(x, by):
    return lax.ppermute(x, "tensor", [(z, (z + by) % RING) for z in range(RING)])


def fetched(x):
    return pl.BlockSpec(x.shape, lambda i: (0,) * x.ndim)


def local_call(body, name, out_shape, operands, scratch=(), fetch=False):
    return pl.pallas_call(
        body,
        out_shape=out_shape,
        grid=(1,) if fetch else (),
        in_specs=[SCALARS] + [fetched(x) if fetch else WHOLE for x in operands[1:]],
        out_specs=jax.tree.map(lambda _: WHOLE, out_shape),
        scratch_shapes=scratch,
        compiler_params=pltpu.CompilerParams(
            vmem_limit_bytes=FETCH_LIMIT if fetch else VMEM_LIMIT
        ),
        cost_estimate=pl.CostEstimate(flops=1, bytes_accessed=1, transcendentals=0),
        name=name,
    )(*operands)


def column(row):
    size = row.shape[1]
    same = lax.broadcasted_iota(jnp.int32, (size, size), 0) == lax.broadcasted_iota(
        jnp.int32, (size, size), 1
    )
    return jnp.sum(jnp.where(same, row, 0.0), axis=1, keepdims=True)


def routes(count_ref, index_ref, gate_ref, token_count):
    size = index_ref.shape[1]
    live = lax.broadcasted_iota(jnp.int32, (1, size), 1) < count_ref[0]
    token = lax.broadcasted_iota(jnp.int32, (token_count, size), 0)
    place = jnp.where(token == index_ref[...], 1.0, 0.0).astype(BF16)
    weight = column(jnp.where(live, gate_ref[...], 0.0))
    return place, weight, column(jnp.where(live, 1.0, 0.0))


def gather_body(count_ref, tokens_ref, grads_ref, index_ref, gate_ref, out_ref):
    token_count, width = tokens_ref.shape
    place, weight, _ = routes(count_ref, index_ref, gate_ref, token_count)
    rows = dot(place, tokens_ref[...], 0, 0).astype(BF16)
    grads = (weight * dot(place, grads_ref[...], 0, 0)).astype(BF16)
    for n in range(CHIPS):
        out_ref[n, :, :width] = rows
        out_ref[n, :, width:] = grads


def pre_body(deltas, where_ref, rows_ref, w_rows_ref, w_grads_ref, payload_ref, *refs):
    here = where_ref[0]
    size = rows_ref.shape[1]
    width = rows_ref.shape[2] // 2
    for n, delta in enumerate(deltas):
        payload_ref[n * size : (n + 1) * size, :] = rows_ref[lax.rem(here + delta, RING)]
    by_rows = dot(payload_ref[:, :width], w_rows_ref[...], 1, 1)
    by_grads = dot(payload_ref[:, width:], w_grads_ref[...], 1, 1)
    mixed = by_rows[:, FIRST:] + by_grads[:, : LAST - FIRST]
    for n, ref in enumerate(refs):
        rows, kind = slice(n * size, (n + 1) * size), ref.dtype
        ref[:, :FIRST] = by_rows[rows, :FIRST].astype(kind)
        ref[:, FIRST:LAST] = mixed[rows].astype(kind)
        ref[:, LAST:] = by_grads[rows, LAST - FIRST :].astype(kind)


def join(refs, to_ref):
    size = refs[0].shape[0]
    for n, ref in enumerate(refs):
        to_ref[n * size : (n + 1) * size, :] = ref[...]


def out_body(where_ref, w_rows_ref, w_grads_ref, *refs):
    keep_ref, give_ref, acts_ref = refs[-3:]
    join(refs[:-3], acts_ref)
    size, width = keep_ref.shape[0], w_rows_ref.shape[1]
    out = dot(acts_ref[:, FIRST:], w_grads_ref[...], 1, 0)
    back = dot(acts_ref[:, :LAST], w_rows_ref[...], 1, 0)
    keep_ref[:, :width] = out[:size]
    keep_ref[:, width:] = back[:size]
    give_ref[:, :width] = out[size:].astype(BF16)
    give_ref[:, width:] = back[size:].astype(BF16)


def weight_body(block, where_ref, *refs):
    dp = where_ref[1]
    payload_refs = refs[:4]
    keep_ref, give_ref, acts_ref = refs[-3:]
    join(refs[4:-3], acts_ref)
    part = keep_ref.shape[0]
    width = 2 * part

    def product(cols, units):
        total, at = None, 0
        for ref in payload_refs:
            term = dot(ref[:, cols], acts_ref[at : at + ref.shape[0], units], 0, 0)
            total = term if total is None else total + term
            at += ref.shape[0]
        return total

    by_rows = product(slice(0, width), slice(0, LAST))
    by_grads = product(slice(width, 2 * width), slice(FIRST, acts_ref.shape[1]))
    unit = FIRST + lax.broadcasted_iota(jnp.int32, (part, LAST - FIRST), 1)
    for cols in (slice(0, FIRST), slice(FIRST, LAST), slice(LAST, acts_ref.shape[1])):
        halves = []
        for rows in (slice(0, part), slice(part, width)):
            if cols.stop == FIRST:
                halves.append(by_rows[rows, :FIRST])
            elif cols.start == FIRST:
                halves.append(
                    jnp.where(
                        unit < 2 * block, by_rows[rows, FIRST:], by_grads[rows, : LAST - FIRST]
                    )
                )
            else:
                halves.append(by_grads[rows, LAST - FIRST :])
        keep_ref[:, cols] = jnp.where(dp == 0, halves[0], halves[1])
        give_ref[:, cols] = jnp.where(dp == 0, halves[1], halves[0]).astype(BF16)


def pair_body(deltas, where_ref, keep_ref, got_ref, keep_last_ref, got_last_ref, out_ref):
    here, x = where_ref[0], where_ref[2]
    size = out_ref.shape[2]

    def place(delta):
        chip = lax.rem(here + delta, RING)
        return lax.rem(lax.div(chip, YS) - x + XS, XS), lax.rem(chip, YS)

    for n, delta in enumerate(deltas):
        rows = slice(n * size, (n + 1) * size)
        out_ref[place(delta)] = (
            keep_ref[rows] + got_ref[rows].astype(F32)
        ).astype(BF16)
    out_ref[place(RING // 2)] = (
        keep_last_ref[...] + got_last_ref[...].astype(F32)
    ).astype(BF16)


def column_body(y_ref, *refs):
    y = y_ref[0]
    stay_ref, leave_ref = refs[-2:]
    stay = sum(ref[y].astype(F32) for ref in refs[:-2])
    leave = sum(ref[1 - y].astype(F32) for ref in refs[:-2])
    stay_ref[...] = stay
    leave_ref[...] = leave.astype(BF16)


def scatter_body(count_ref, stay_ref, got_ref, index_ref, gate_ref, mixed_ref, grad_ref):
    total = stay_ref[...] + got_ref[...].astype(F32)
    token_count, width = mixed_ref.shape
    place, weight, live = routes(count_ref, index_ref, gate_ref, token_count)
    out_rows = (weight * total[:, :width]).astype(BF16)
    back_rows = jnp.where(live > 0.0, total[:, width:], 0.0).astype(BF16)
    mixed_ref[...] = dot(place, out_rows, 1, 0).astype(BF16)
    grad_ref[...] = dot(place, back_rows, 1, 0).astype(BF16)


def on_device(
    tokens, out_grad, gate_weight, up_weight, down_weight, route_count, route_index, route_gate
):
    capacity = route_index.shape[0]
    token_count, width = tokens.shape
    block = gate_weight.shape[0]
    units = 3 * block
    here = lax.axis_index("tensor")
    where = jnp.stack([here, lax.axis_index("dp"), lax.axis_index("x")]).astype(jnp.int32)
    routing = [route_index[None, :], route_gate[None, :]]

    w_rows = jnp.concatenate(
        [gate_weight, up_weight, jnp.zeros((LAST - 2 * block, width), BF16)], axis=0
    )
    w_grads = jnp.concatenate(
        [jnp.zeros((2 * block - FIRST, width), BF16), down_weight], axis=0
    )

    copies = local_call(
        gather_body,
        "gather_rows",
        jax.ShapeDtypeStruct((CHIPS, capacity, 2 * width), BF16),
        [route_count, tokens, out_grad] + routing,
        fetch=True,
    )
    came = among_chips(copies)
    rows = [came, core_swap(came)]
    pre = {}
    payloads = []
    first, rest = (4, 3, 5), (2, 6, 1, 7, 0)
    for deltas, name in ((first, "pre_first"), (rest, "pre_rest")):
        for h in range(2):
            shapes = [jax.ShapeDtypeStruct((len(deltas) * capacity, 2 * width), BF16)]
            for delta in deltas:
                starts = delta == 4 or (delta, h) in ((3, 0), (5, 1))
                shapes.append(jax.ShapeDtypeStruct((capacity, units), BF16 if starts else F32))
            payload, *blocks = local_call(
                functools.partial(pre_body, deltas),
                name,
                shapes,
                [where, rows[h], w_rows, w_grads],
            )
            payloads.append(payload)
            pre.update({(delta, h): part for delta, part in zip(deltas, blocks)})
        if deltas is first:
            rows[0], payloads[1] = lax.optimization_barrier((rows[0], payloads[1]))

    own_left, own_right = ring(pre[4, 0], -1), ring(pre[3, 0], 1)
    own_left, own_right, payloads[1] = lax.optimization_barrier(
        (own_left, own_right, payloads[1])
    )
    sums = []
    for h, ways in (
        (0, ((own_left, (5, 6, 7), -1), (own_right, (2, 1), 1))),
        (1, ((None, (5, 6, 7), -1), (None, (4, 3, 2, 1), 1))),
    ):
        total = pre[0, h]
        for moving, path, by in ways:
            for delta in path:
                block_sum = pre[delta, h]
                if moving is not None:
                    block_sum = block_sum + moving.astype(F32)
                moving = ring(block_sum.astype(BF16), by)
            total = total + moving.astype(F32)
        sums.append(total)

    acts_own = []
    for total in sums:
        gate_pre, up_pre, d_hidden = (
            total[:, :block],
            total[:, block : 2 * block],
            total[:, 2 * block :],
        )
        sigmoid_gate = jax.nn.sigmoid(gate_pre)
        activated = gate_pre * sigmoid_gate
        hidden = (activated * up_pre).astype(BF16)
        d_gate = (
            d_hidden * up_pre * sigmoid_gate * (1.0 + gate_pre * (1.0 - sigmoid_gate))
        ).astype(BF16)
        d_up = (d_hidden * activated).astype(BF16)
        acts_own.append(jnp.concatenate([d_gate, d_up, hidden], axis=1))

    halves = {0: acts_own}
    right = list(acts_own)
    left = list(acts_own)
    for step in (1, 2, 3):
        right = [ring(a, 1) for a in right]
        left = [ring(a, -1) for a in left]
        halves[RING - step] = right
        halves[step] = left
    halves[4] = [ring(right[0], 1), ring(left[1], -1)]

    near, far = (0, 7, 1, 6, 2, 5, 3), (4,)
    kept, given = [], []
    for deltas, name in ((near, "out_near"), (far, "out_far")):
        shape = (len(deltas) * capacity, 2 * width)
        keep, give = local_call(
            out_body,
            name,
            [jax.ShapeDtypeStruct(shape, F32), jax.ShapeDtypeStruct(shape, BF16)],
            [where, w_rows, w_grads] + [halves[delta][h] for h in range(2) for delta in deltas],
            [pltpu.VMEM((2 * len(deltas) * capacity, units), BF16)],
        )
        kept.append(keep)
        given.append(give)
    swapped = [core_swap(give) for give in lax.optimization_barrier(given)]

    part = width // 2
    pieces = [halves[delta][h] for deltas in (first, rest) for h in range(2) for delta in deltas]
    keep_w, give_w = local_call(
        functools.partial(weight_body, block),
        "weight_grads",
        [jax.ShapeDtypeStruct((part, units), F32), jax.ShapeDtypeStruct((part, units), BF16)],
        [where] + payloads + pieces,
        [pltpu.VMEM((len(pieces) * capacity, units), BF16)],
    )
    swapped, give_w = lax.optimization_barrier((swapped, give_w))
    got_w = lax.ppermute(give_w, "dp", [(0, 1), (1, 0)])
    by_chip = local_call(
        functools.partial(pair_body, near),
        "pair_sum",
        jax.ShapeDtypeStruct((XS, YS, capacity, 2 * width), BF16),
        [where, kept[0], swapped[0], kept[1], swapped[1]],
    )
    along = [by_chip[0]] + [along_x(by_chip[by], by) for by in (1, 3, 2)]
    stay, leave = local_call(
        column_body,
        "x_sum",
        [
            jax.ShapeDtypeStruct((capacity, 2 * width), F32),
            jax.ShapeDtypeStruct((capacity, 2 * width), BF16),
        ],
        [lax.axis_index("y")[None].astype(jnp.int32)] + along,
    )
    arrived = (stay, lax.ppermute(leave, "y", [(0, 1), (1, 0)]))
    mixed, input_grad = local_call(
        scatter_body,
        "scatter_rows",
        [jax.ShapeDtypeStruct((token_count, width), BF16)] * 2,
        [route_count, *arrived] + routing,
    )
    grads_w = keep_w + got_w.astype(F32)
    return (
        mixed,
        input_grad,
        grads_w[:, :block].T,
        grads_w[:, block : 2 * block].T,
        grads_w[:, 2 * block :].T,
    )


def solution(mesh):
    ways = (("x", "y", "core"), "tensor", "dp")
    chips = Mesh(mesh.devices.reshape(XS, YS, CORES, RING, 2), ways[0] + ways[1:])
    expert, tensor, dp = ways
    tokens = P(expert + (dp,), tensor)
    weight = P(expert, tensor)
    slots = P(expert + (dp,))
    grad = P(expert, (tensor, dp))
    return jax.shard_map(
        on_device,
        mesh=chips,
        in_specs=(tokens, tokens, weight, weight, weight, slots, slots, slots),
        out_specs=(tokens, tokens, grad, grad, grad),
        check_vma=False,
    )
```

profile of v0, /device:TPU:1, one launch (start us, length us, event | category | flops | bytes accessed | tf_op | source)
XLA Modules:
  0.0 140.3 jit_solution(13043658911085909350)
XLA Ops:
  1.3 2.4 %gather_rows.1 = bf16[8,96,768]{2,1,0:T(8,128)(2,1)} custom-call(s32[1]{0:T(128)S(6)} %copy.13.count_ref, bf16[256,384]{1,0:T(8,128)(2,1)} %tokens_ref.1, bf16[256,384]{1,0:T(8,128)(2,1)} %grads_ref.1, s32[1,96]{1,0:T(1,128)} %bitcast.20, f32[1,96]{1,0:T(1,128)} %bitcast.22), custom_call_target="tpu_custom_call" | custom-call | flops 1 | bytes 1 | tf_op jit(solution)/shard_map/gather_rows/pallas_call | solution.py:49
  3.7 24.6 %all_to_all.5.rows_ref = bf16[8,96,768]{2,1,0:T(8,128)(2,1)S(1)} all-to-all(bf16[8,96,768]{2,1,0:T(8,128)(2,1)} %gather_rows.1), channel_id=1, replica_groups=mesh['x'=4,'y'=2,'core'=2,'tensor'=8,'dp'=2] {'x','y'}, dimensions={0} | all-to-all | bytes 2359296 | tf_op jit(solution)/shard_map/all_to_all | solution.py:33
  28.3 2.4 %collective-permute-start = (bf16[8,96,768]{2,1,0:T(8,128)(2,1)S(1)}, bf16[8,96,768]{2,1,0:T(8,128)(2,1)S(1)}, u32[]{:S(2)}, u32[]{:S(2)}) collective-permute-start(bf16[8,96,768]{2,1,0:T(8,128)(2,1)S(1)} %all_to_all.5.rows_ref), channel_id=1, source_target_pairs={{0,16},{16,0},{1,17},{17,1},{2,18},{18,2},{3,19},{19,3},{4,20},{20... | collective-permute-start | bytes 3538952 | tf_op jit(solution)/shard_map/ppermute | solution.py:29
  32.2 5.7 %collective-permute-start.1 = (bf16[96,1008]{1,0:T(8,128)(2,1)S(1)}, bf16[96,1008]{1,0:T(8,128)(2,1)S(1)}, u32[]{:S(2)}, u32[]{:S(2)}) collective-permute-start(bf16[96,1008]{1,0:T(8,128)(2,1)S(1)} %get-tuple-element.51), channel_id=1, source_target_pairs={{0,14},{2,0},{4,2},{6,4},{8,6},{10,8},{12,10},{14,12},{1,15},{3,1}... | collective-permute-start | bytes 580616 | tf_op jit(solution)/shard_map/ppermute | solution.py:41
  39.0 2.7 %collective-permute-start.14 = (bf16[96,1008]{1,0:T(8,128)(2,1)S(1)}, bf16[96,1008]{1,0:T(8,128)(2,1)S(1)}, u32[]{:S(2)}, u32[]{:S(2)}) collective-permute-start(bf16[96,1008]{1,0:T(8,128)(2,1)S(1)} %get-tuple-element.61), channel_id=1, source_target_pairs={{0,14},{2,0},{4,2},{6,4},{8,6},{10,8},{12,10},{14,12},{1,15},{3,1}... | collective-permute-start | bytes 580616 | tf_op jit(solution)/shard_map/ppermute | solution.py:41
  42.2 3.1 %collective-permute-done.2 = bf16[96,1008]{1,0:T(8,128)(2,1)S(1)} collective-permute-done((bf16[96,1008]{1,0:T(8,128)(2,1)S(1)}, bf16[96,1008]{1,0:T(8,128)(2,1)S(1)}, u32[]{:S(2)}, u32[]{:S(2)}) %collective-permute-start.2) | collective-permute-done | bytes 193568 | tf_op jit(solution)/shard_map/ppermute | solution.py:41
  50.5 3.0 %collective-permute-start.4 = (bf16[96,1008]{1,0:T(8,128)(2,1)S(1)}, bf16[96,1008]{1,0:T(8,128)(2,1)S(1)}, u32[]{:S(2)}, u32[]{:S(2)}) collective-permute-start(bf16[96,1008]{1,0:T(8,128)(2,1)S(1)} %add_convert_fusion.8), channel_id=1, source_target_pairs={{0,14},{2,0},{4,2},{6,4},{8,6},{10,8},{12,10},{14,12},{1,15},{3,1}... | collective-permute-start | bytes 580616 | tf_op jit(solution)/shard_map/ppermute | solution.py:41
  53.7 2.7 %collective-permute-start.15 = (bf16[96,1008]{1,0:T(8,128)(2,1)S(1)}, bf16[96,1008]{1,0:T(8,128)(2,1)S(1)}, u32[]{:S(2)}, u32[]{:S(2)}) collective-permute-start(bf16[96,1008]{1,0:T(8,128)(2,1)S(1)} %add_convert_fusion.4), channel_id=1, source_target_pairs={{0,14},{2,0},{4,2},{6,4},{8,6},{10,8},{12,10},{14,12},{1,15},{3,1}... | collective-permute-start | bytes 580616 | tf_op jit(solution)/shard_map/ppermute | solution.py:41
  56.5 3.5 %collective-permute-start.5 = (bf16[96,1008]{1,0:T(8,128)(2,1)S(1)}, bf16[96,1008]{1,0:T(8,128)(2,1)S(1)}, u32[]{:S(2)}, u32[]{:S(2)}) collective-permute-start(bf16[96,1008]{1,0:T(8,128)(2,1)S(1)} %add_convert_fusion.7), channel_id=1, source_target_pairs={{0,14},{2,0},{4,2},{6,4},{8,6},{10,8},{12,10},{14,12},{1,15},{3,1}... | collective-permute-start | bytes 580616 | tf_op jit(solution)/shard_map/ppermute | solution.py:41
  60.4 3.2 %collective-permute-start.16 = (bf16[96,1008]{1,0:T(8,128)(2,1)S(1)}, bf16[96,1008]{1,0:T(8,128)(2,1)S(1)}, u32[]{:S(2)}, u32[]{:S(2)}) collective-permute-start(bf16[96,1008]{1,0:T(8,128)(2,1)S(1)} %add_convert_fusion.3), channel_id=1, source_target_pairs={{0,14},{2,0},{4,2},{6,4},{8,6},{10,8},{12,10},{14,12},{1,15},{3,1}... | collective-permute-start | bytes 580616 | tf_op jit(solution)/shard_map/ppermute | solution.py:41
  63.6 2.3 %collective-permute-done.19 = bf16[96,1008]{1,0:T(8,128)(2,1)S(1)} collective-permute-done((bf16[96,1008]{1,0:T(8,128)(2,1)S(1)}, bf16[96,1008]{1,0:T(8,128)(2,1)S(1)}, u32[]{:S(2)}, u32[]{:S(2)}) %collective-permute-start.19) | collective-permute-done | bytes 193568 | tf_op jit(solution)/shard_map/ppermute | solution.py:41
  68.4 4.0 %collective-permute-done.20 = bf16[96,1008]{1,0:T(8,128)(2,1)S(1)} collective-permute-done((bf16[96,1008]{1,0:T(8,128)(2,1)S(1)}, bf16[96,1008]{1,0:T(8,128)(2,1)S(1)}, u32[]{:S(2)}, u32[]{:S(2)}) %collective-permute-start.20) | collective-permute-done | bytes 193568 | tf_op jit(solution)/shard_map/ppermute | solution.py:41
  81.2 2.9 %collective-permute-done.10.refs_3_.refs_11_ = bf16[96,1008]{1,0:T(8,128)(2,1)S(1)} collective-permute-done((bf16[96,1008]{1,0:T(8,128)(2,1)S(1)}, bf16[96,1008]{1,0:T(8,128)(2,1)S(1)}, u32[]{:S(2)}, u32[]{:S(2)}) %collective-permute-start.10) | collective-permute-done | bytes 193568 | tf_op jit(solution)/shard_map/ppermute | solution.py:41
  84.1 2.7 %collective-permute-start.26 = (bf16[96,1008]{1,0:T(8,128)(2,1)S(1)}, bf16[96,1008]{1,0:T(8,128)(2,1)S(1)}, u32[]{:S(2)}, u32[]{:S(2)}) collective-permute-start(bf16[96,1008]{1,0:T(8,128)(2,1)S(1)} %collective-permute-done.24.refs_11_.refs_15_), channel_id=1, source_target_pairs={{0,14},{2,0},{4,2},{6,4},{8,6},{10,8},{12,10},{14,12},{1,15},{3,1}... | collective-permute-start | bytes 580616 | tf_op jit(solution)/shard_map/ppermute | solution.py:41
  89.2 3.6 %collective-permute-done.12.refs_5_.refs_6_ = bf16[96,1008]{1,0:T(8,128)(2,1)S(1)} collective-permute-done((bf16[96,1008]{1,0:T(8,128)(2,1)S(1)}, bf16[96,1008]{1,0:T(8,128)(2,1)S(1)}, u32[]{:S(2)}, u32[]{:S(2)}) %collective-permute-start.12) | collective-permute-done | bytes 193568 | tf_op jit(solution)/shard_map/ppermute | solution.py:41
  92.8 2.7 %collective-permute-start.28 = (bf16[96,1008]{1,0:T(8,128)(2,1)S(1)}, bf16[96,1008]{1,0:T(8,128)(2,1)S(1)}, u32[]{:S(2)}, u32[]{:S(2)}) collective-permute-start(bf16[96,1008]{1,0:T(8,128)(2,1)S(1)} %collective-permute-done.26.refs_13_.refs_8_), channel_id=1, source_target_pairs={{0,14},{2,0},{4,2},{6,4},{8,6},{10,8},{12,10},{14,12},{1,15},{3,1}... | collective-permute-start | bytes 580616 | tf_op jit(solution)/shard_map/ppermute | solution.py:41
  95.5 2.4 %out_near.1 = (f32[672,768]{1,0:T(8,128)S(1)}, bf16[672,768]{1,0:T(8,128)(2,1)S(1)}) custom-call(s32[3]{0:T(128)S(1)} %pad_add_fusion.where_ref, bf16[768,384]{1,0:T(8,128)(2,1)S(1)} %maximum_maximum_fusion.w_rows_ref, bf16[368,384]{1,0:T(8,128)(2,1)S(1)} %concatenate.13.w_grads_ref, bf16[96,1008]{1,0:T(8,128)(2,1)S(1)} %pad_maximum_fusion.refs_0_.refs_14_, ...), custom_call_target="tpu_custom_call" | custom-call | flops 1 | bytes 1 | tf_op jit(solution)/shard_map/out_near/pallas_call | solution.py:49
  97.9 3.0 %collective-permute-done.27.refs_0_.refs_4_ = bf16[96,1008]{1,0:T(8,128)(2,1)S(1)} collective-permute-done((bf16[96,1008]{1,0:T(8,128)(2,1)S(1)}, bf16[96,1008]{1,0:T(8,128)(2,1)S(1)}, u32[]{:S(2)}, u32[]{:S(2)}) %collective-permute-start.27) | collective-permute-done | bytes 193568 | tf_op jit(solution)/shard_map/ppermute | solution.py:41
  101.8 8.8 %collective-permute-start.29 = (bf16[672,768]{1,0:T(8,128)(2,1)S(1)}, bf16[672,768]{1,0:T(8,128)(2,1)S(1)}, u32[]{:S(2)}, u32[]{:S(2)}) collective-permute-start(bf16[672,768]{1,0:T(8,128)(2,1)S(1)} %get-tuple-element.69), channel_id=1, source_target_pairs={{0,16},{16,0},{1,17},{17,1},{2,18},{18,2},{3,19},{19,3},{4,20},{20... | collective-permute-start | bytes 3096584 | tf_op jit(solution)/shard_map/ppermute | solution.py:29
  110.7 2.8 %weight_grads.1 = (f32[192,1008]{1,0:T(8,128)S(1)}, bf16[192,1008]{1,0:T(8,128)(2,1)S(1)}) custom-call(s32[3]{0:T(128)S(1)} %pad_add_fusion.where_ref, bf16[288,768]{1,0:T(8,128)(2,1)S(1)} %get-tuple-element.71.refs_0_, bf16[288,768]{1,0:T(8,128)(2,1)S(1)} %get-tuple-element.72.refs_1_, bf16[480,768]{1,0:T(8,128)(2,1)S(1)} %get-tuple-element.73.refs_2_, ...), custom_call_target="tpu_custom_call" | custom-call | flops 1 | bytes 1 | tf_op jit(solution)/shard_map/weight_grads/pallas_call | solution.py:49
  118.4 6.9 %collective-permute-done.33.refs_3_ = bf16[2,96,768]{2,1,0:T(8,128)(2,1)S(1)} collective-permute-done((bf16[2,96,768]{2,1,0:T(8,128)(2,1)}, bf16[2,96,768]{2,1,0:T(8,128)(2,1)S(1)}, u32[]{:S(2)}, u32[]{:S(2)}) %collective-permute-start.33) | collective-permute-done | bytes 294944 | tf_op jit(solution)/shard_map/ppermute | solution.py:37
  125.2 4.8 %collective-permute-done.32.refs_2_ = bf16[2,96,768]{2,1,0:T(8,128)(2,1)S(1)} collective-permute-done((bf16[2,96,768]{2,1,0:T(8,128)(2,1)S(1)}, bf16[2,96,768]{2,1,0:T(8,128)(2,1)S(1)}, u32[]{:S(2)}, u32[]{:S(2)}) %collective-permute-start.32) | collective-permute-done | bytes 294944 | tf_op jit(solution)/shard_map/ppermute | solution.py:37
  130.1 2.5 %collective-permute-done.31.refs_1_ = bf16[2,96,768]{2,1,0:T(8,128)(2,1)S(1)} collective-permute-done((bf16[2,96,768]{2,1,0:T(8,128)(2,1)S(1)}, bf16[2,96,768]{2,1,0:T(8,128)(2,1)S(1)}, u32[]{:S(2)}, u32[]{:S(2)}) %collective-permute-start.31) | collective-permute-done | bytes 294944 | tf_op jit(solution)/shard_map/ppermute | solution.py:37
  135.5 3.8 %collective-permute-done.34.got_ref = bf16[96,768]{1,0:T(8,128)(2,1)S(1)} collective-permute-done((bf16[96,768]{1,0:T(8,128)(2,1)S(1)}, bf16[96,768]{1,0:T(8,128)(2,1)S(1)}, u32[]{:S(2)}, u32[]{:S(2)}) %collective-permute-start.34) | collective-permute-done | bytes 147488 | tf_op jit(solution)/shard_map/ppermute | solution.py:332
  (94 shorter events, 32.2 us)
Async XLA Ops:
  28.3 9.6 %collective-permute-start = (bf16[8,96,768]{2,1,0:T(8,128)(2,1)S(1)}, bf16[8,96,768]{2,1,0:T(8,128)(2,1)S(1)}, u32[]{:S(2)}, u32[]{:S(2)}) collective-permute-start(bf16[8,96,768]{2,1,0:T(8,128)(2,1)S(1)} %all_to_all.5.rows_ref), channel_id=1, source_target_pairs={{0,16},{16,0},{1,17},{17,1},{2,18},{18,2},{3,19},{19,3},{4,20},{20... | collective-permute-start | bytes 3538952 | tf_op jit(solution)/shard_map/ppermute | solution.py:29
  32.2 10.0 %collective-permute-start.1 = (bf16[96,1008]{1,0:T(8,128)(2,1)S(1)}, bf16[96,1008]{1,0:T(8,128)(2,1)S(1)}, u32[]{:S(2)}, u32[]{:S(2)}) collective-permute-start(bf16[96,1008]{1,0:T(8,128)(2,1)S(1)} %get-tuple-element.51), channel_id=1, source_target_pairs={{0,14},{2,0},{4,2},{6,4},{8,6},{10,8},{12,10},{14,12},{1,15},{3,1}... | collective-permute-start | bytes 580616 | tf_op jit(solution)/shard_map/ppermute | solution.py:41
  37.9 7.4 %collective-permute-start.2 = (bf16[96,1008]{1,0:T(8,128)(2,1)S(1)}, bf16[96,1008]{1,0:T(8,128)(2,1)S(1)}, u32[]{:S(2)}, u32[]{:S(2)}) collective-permute-start(bf16[96,1008]{1,0:T(8,128)(2,1)S(1)} %get-tuple-element.52), channel_id=1, source_target_pairs={{0,2},{2,4},{4,6},{6,8},{8,10},{10,12},{12,14},{14,0},{1,3},{3,5},... | collective-permute-start | bytes 580616 | tf_op jit(solution)/shard_map/ppermute | solution.py:41
  39.0 14.7 %collective-permute-start.14 = (bf16[96,1008]{1,0:T(8,128)(2,1)S(1)}, bf16[96,1008]{1,0:T(8,128)(2,1)S(1)}, u32[]{:S(2)}, u32[]{:S(2)}) collective-permute-start(bf16[96,1008]{1,0:T(8,128)(2,1)S(1)} %get-tuple-element.61), channel_id=1, source_target_pairs={{0,14},{2,0},{4,2},{6,4},{8,6},{10,8},{12,10},{14,12},{1,15},{3,1}... | collective-permute-start | bytes 580616 | tf_op jit(solution)/shard_map/ppermute | solution.py:41
  41.7 8.0 %collective-permute-start.17 = (bf16[96,1008]{1,0:T(8,128)(2,1)S(1)}, bf16[96,1008]{1,0:T(8,128)(2,1)S(1)}, u32[]{:S(2)}, u32[]{:S(2)}) collective-permute-start(bf16[96,1008]{1,0:T(8,128)(2,1)S(1)} %get-tuple-element.65), channel_id=1, source_target_pairs={{0,2},{2,4},{4,6},{6,8},{8,10},{10,12},{12,14},{14,0},{1,3},{3,5},... | collective-permute-start | bytes 580616 | tf_op jit(solution)/shard_map/ppermute | solution.py:41
  49.8 10.3 %collective-permute-start.18 = (bf16[96,1008]{1,0:T(8,128)(2,1)S(1)}, bf16[96,1008]{1,0:T(8,128)(2,1)S(1)}, u32[]{:S(2)}, u32[]{:S(2)}) collective-permute-start(bf16[96,1008]{1,0:T(8,128)(2,1)S(1)} %add_convert_fusion.2), channel_id=1, source_target_pairs={{0,2},{2,4},{4,6},{6,8},{8,10},{10,12},{12,14},{14,0},{1,3},{3,5},... | collective-permute-start | bytes 580616 | tf_op jit(solution)/shard_map/ppermute | solution.py:41
  53.6 12.4 %collective-permute-start.7 = (bf16[96,1008]{1,0:T(8,128)(2,1)S(1)}, bf16[96,1008]{1,0:T(8,128)(2,1)S(1)}, u32[]{:S(2)}, u32[]{:S(2)}) collective-permute-start(bf16[96,1008]{1,0:T(8,128)(2,1)S(1)} %add_convert_fusion.5), channel_id=1, source_target_pairs={{0,2},{2,4},{4,6},{6,8},{8,10},{10,12},{12,14},{14,0},{1,3},{3,5},... | collective-permute-start | bytes 580616 | tf_op jit(solution)/shard_map/ppermute | solution.py:41
  56.5 9.5 %collective-permute-start.5 = (bf16[96,1008]{1,0:T(8,128)(2,1)S(1)}, bf16[96,1008]{1,0:T(8,128)(2,1)S(1)}, u32[]{:S(2)}, u32[]{:S(2)}) collective-permute-start(bf16[96,1008]{1,0:T(8,128)(2,1)S(1)} %add_convert_fusion.7), channel_id=1, source_target_pairs={{0,14},{2,0},{4,2},{6,4},{8,6},{10,8},{12,10},{14,12},{1,15},{3,1}... | collective-permute-start | bytes 580616 | tf_op jit(solution)/shard_map/ppermute | solution.py:41
  60.4 8.0 %collective-permute-start.16 = (bf16[96,1008]{1,0:T(8,128)(2,1)S(1)}, bf16[96,1008]{1,0:T(8,128)(2,1)S(1)}, u32[]{:S(2)}, u32[]{:S(2)}) collective-permute-start(bf16[96,1008]{1,0:T(8,128)(2,1)S(1)} %add_convert_fusion.3), channel_id=1, source_target_pairs={{0,14},{2,0},{4,2},{6,4},{8,6},{10,8},{12,10},{14,12},{1,15},{3,1}... | collective-permute-start | bytes 580616 | tf_op jit(solution)/shard_map/ppermute | solution.py:41
  66.4 8.1 %collective-permute-start.8 = (bf16[96,1008]{1,0:T(8,128)(2,1)S(1)}, bf16[96,1008]{1,0:T(8,128)(2,1)S(1)}, u32[]{:S(2)}, u32[]{:S(2)}) collective-permute-start(bf16[96,1008]{1,0:T(8,128)(2,1)S(1)} %pad_maximum_fusion.refs_0_.refs_14_), channel_id=1, source_target_pairs={{0,2},{2,4},{4,6},{6,8},{8,10},{10,12},{12,14},{14,0},{1,3},{3,5},... | collective-permute-start | bytes 580616 | tf_op jit(solution)/shard_map/ppermute | solution.py:41
  72.9 8.2 %collective-permute-start.21 = (bf16[96,1008]{1,0:T(8,128)(2,1)S(1)}, bf16[96,1008]{1,0:T(8,128)(2,1)S(1)}, u32[]{:S(2)}, u32[]{:S(2)}) collective-permute-start(bf16[96,1008]{1,0:T(8,128)(2,1)S(1)} %pad_maximum_fusion.1.refs_7_.refs_19_), channel_id=1, source_target_pairs={{0,2},{2,4},{4,6},{6,8},{8,10},{10,12},{12,14},{14,0},{1,3},{3,5},... | collective-permute-start | bytes 580616 | tf_op jit(solution)/shard_map/ppermute | solution.py:41
  74.5 9.6 %collective-permute-start.10 = (bf16[96,1008]{1,0:T(8,128)(2,1)S(1)}, bf16[96,1008]{1,0:T(8,128)(2,1)S(1)}, u32[]{:S(2)}, u32[]{:S(2)}) collective-permute-start(bf16[96,1008]{1,0:T(8,128)(2,1)S(1)} %collective-permute-done.8.refs_1_.refs_13_), channel_id=1, source_target_pairs={{0,2},{2,4},{4,6},{6,8},{8,10},{10,12},{12,14},{14,0},{1,3},{3,5},... | collective-permute-start | bytes 580616 | tf_op jit(solution)/shard_map/ppermute | solution.py:41
  79.7 7.1 %collective-permute-start.11 = (bf16[96,1008]{1,0:T(8,128)(2,1)S(1)}, bf16[96,1008]{1,0:T(8,128)(2,1)S(1)}, u32[]{:S(2)}, u32[]{:S(2)}) collective-permute-start(bf16[96,1008]{1,0:T(8,128)(2,1)S(1)} %collective-permute-done.9.refs_2_.refs_12_), channel_id=1, source_target_pairs={{0,14},{2,0},{4,2},{6,4},{8,6},{10,8},{12,10},{14,12},{1,15},{3,1}... | collective-permute-start | bytes 580616 | tf_op jit(solution)/shard_map/ppermute | solution.py:41
  81.1 8.1 %collective-permute-start.23 = (bf16[96,1008]{1,0:T(8,128)(2,1)S(1)}, bf16[96,1008]{1,0:T(8,128)(2,1)S(1)}, u32[]{:S(2)}, u32[]{:S(2)}) collective-permute-start(bf16[96,1008]{1,0:T(8,128)(2,1)S(1)} %collective-permute-done.21.refs_8_.refs_18_), channel_id=1, source_target_pairs={{0,2},{2,4},{4,6},{6,8},{8,10},{10,12},{12,14},{14,0},{1,3},{3,5},... | collective-permute-start | bytes 580616 | tf_op jit(solution)/shard_map/ppermute | solution.py:41
  84.1 8.7 %collective-permute-start.12 = (bf16[96,1008]{1,0:T(8,128)(2,1)S(1)}, bf16[96,1008]{1,0:T(8,128)(2,1)S(1)}, u32[]{:S(2)}, u32[]{:S(2)}) collective-permute-start(bf16[96,1008]{1,0:T(8,128)(2,1)S(1)} %collective-permute-done.10.refs_3_.refs_11_), channel_id=1, source_target_pairs={{0,2},{2,4},{4,6},{6,8},{8,10},{10,12},{12,14},{14,0},{1,3},{3,5},... | collective-permute-start | bytes 580616 | tf_op jit(solution)/shard_map/ppermute | solution.py:41
  84.1 8.7 %collective-permute-start.26 = (bf16[96,1008]{1,0:T(8,128)(2,1)S(1)}, bf16[96,1008]{1,0:T(8,128)(2,1)S(1)}, u32[]{:S(2)}, u32[]{:S(2)}) collective-permute-start(bf16[96,1008]{1,0:T(8,128)(2,1)S(1)} %collective-permute-done.24.refs_11_.refs_15_), channel_id=1, source_target_pairs={{0,14},{2,0},{4,2},{6,4},{8,6},{10,8},{12,10},{14,12},{1,15},{3,1}... | collective-permute-start | bytes 580616 | tf_op jit(solution)/shard_map/ppermute | solution.py:41
  86.8 8.7 %collective-permute-start.13 = (bf16[96,1008]{1,0:T(8,128)(2,1)S(1)}, bf16[96,1008]{1,0:T(8,128)(2,1)S(1)}, u32[]{:S(2)}, u32[]{:S(2)}) collective-permute-start(bf16[96,1008]{1,0:T(8,128)(2,1)S(1)} %collective-permute-done.11.refs_4_.refs_10_), channel_id=1, source_target_pairs={{0,14},{2,0},{4,2},{6,4},{8,6},{10,8},{12,10},{14,12},{1,15},{3,1}... | collective-permute-start | bytes 580616 | tf_op jit(solution)/shard_map/ppermute | solution.py:41
  92.8 8.1 %collective-permute-start.27 = (bf16[96,1008]{1,0:T(8,128)(2,1)S(1)}, bf16[96,1008]{1,0:T(8,128)(2,1)S(1)}, u32[]{:S(2)}, u32[]{:S(2)}) collective-permute-start(bf16[96,1008]{1,0:T(8,128)(2,1)S(1)} %collective-permute-done.12.refs_5_.refs_6_), channel_id=1, source_target_pairs={{0,2},{2,4},{4,6},{6,8},{8,10},{10,12},{12,14},{14,0},{1,3},{3,5},... | collective-permute-start | bytes 580616 | tf_op jit(solution)/shard_map/ppermute | solution.py:41
  92.8 8.1 %collective-permute-start.28 = (bf16[96,1008]{1,0:T(8,128)(2,1)S(1)}, bf16[96,1008]{1,0:T(8,128)(2,1)S(1)}, u32[]{:S(2)}, u32[]{:S(2)}) collective-permute-start(bf16[96,1008]{1,0:T(8,128)(2,1)S(1)} %collective-permute-done.26.refs_13_.refs_8_), channel_id=1, source_target_pairs={{0,14},{2,0},{4,2},{6,4},{8,6},{10,8},{12,10},{14,12},{1,15},{3,1}... | collective-permute-start | bytes 580616 | tf_op jit(solution)/shard_map/ppermute | solution.py:41
  101.8 11.7 %collective-permute-start.29 = (bf16[672,768]{1,0:T(8,128)(2,1)S(1)}, bf16[672,768]{1,0:T(8,128)(2,1)S(1)}, u32[]{:S(2)}, u32[]{:S(2)}) collective-permute-start(bf16[672,768]{1,0:T(8,128)(2,1)S(1)} %get-tuple-element.69), channel_id=1, source_target_pairs={{0,16},{16,0},{1,17},{17,1},{2,18},{18,2},{3,19},{19,3},{4,20},{20... | collective-permute-start | bytes 3096584 | tf_op jit(solution)/shard_map/ppermute | solution.py:29
  113.6 20.6 %collective-permute-start.35 = (bf16[192,1008]{1,0:T(8,128)(2,1)S(1)}, bf16[192,1008]{1,0:T(8,128)(2,1)S(1)}, u32[]{:S(2)}, u32[]{:S(2)}) collective-permute-start(bf16[192,1008]{1,0:T(8,128)(2,1)S(1)} %get-tuple-element.84), channel_id=1, source_target_pairs={{0,1},{1,0},{2,3},{3,2},{4,5},{5,4},{6,7},{7,6},{8,9},{9,8},{10,11... | collective-permute-start | bytes 1161224 | tf_op jit(solution)/shard_map/ppermute | solution.py:315
  115.6 9.6 %collective-permute-start.33 = (bf16[2,96,768]{2,1,0:T(8,128)(2,1)}, bf16[2,96,768]{2,1,0:T(8,128)(2,1)S(1)}, u32[]{:S(2)}, u32[]{:S(2)}) collective-permute-start(bf16[2,96,768]{2,1,0:T(8,128)(2,1)} %get-tuple-element.85), channel_id=1, source_target_pairs={{0,128},{64,192},{128,0},{192,64},{1,129},{65,193},{129,1},{193,65... | collective-permute-start | bytes 884744 | tf_op jit(solution)/shard_map/ppermute | solution.py:37
  116.9 13.2 %collective-permute-start.32 = (bf16[2,96,768]{2,1,0:T(8,128)(2,1)S(1)}, bf16[2,96,768]{2,1,0:T(8,128)(2,1)S(1)}, u32[]{:S(2)}, u32[]{:S(2)}) collective-permute-start(bf16[2,96,768]{2,1,0:T(8,128)(2,1)S(1)} %get-tuple-element.86), channel_id=1, source_target_pairs={{0,192},{64,0},{128,64},{192,128},{1,193},{65,1},{129,65},{193,129... | collective-permute-start | bytes 884744 | tf_op jit(solution)/shard_map/ppermute | solution.py:37
  118.3 14.2 %collective-permute-start.31 = (bf16[2,96,768]{2,1,0:T(8,128)(2,1)S(1)}, bf16[2,96,768]{2,1,0:T(8,128)(2,1)S(1)}, u32[]{:S(2)}, u32[]{:S(2)}) collective-permute-start(bf16[2,96,768]{2,1,0:T(8,128)(2,1)S(1)} %get-tuple-element.87), channel_id=1, source_target_pairs={{0,64},{64,128},{128,192},{192,0},{1,65},{65,129},{129,193},{193,1... | collective-permute-start | bytes 884744 | tf_op jit(solution)/shard_map/ppermute | solution.py:37
  (17 other events, 162.0 us)
where the time goes:
time: 140 us
  starting transfers between devices  51.4 us (37%)
  waiting for transfers between devices  43.8 us (31%)
  blocking collectives  24.6 us (18%)
  Pallas kernels  15.4 us (11%)
  local copies, waits for them, and re-layouts  2.04 us (1%)
  between operations  1.61 us (1%)
  other arithmetic  1.46 us (1%)
    ppermute x28, starting transfers between devices, ring(): lax.ppermute(x, 'tensor', [(z, (z + by) % RING) for z in range(RING)])  35.3 us
    ppermute x28, waiting for transfers between devices, ring(): lax.ppermute(x, 'tensor', [(z, (z + by) % RING) for z in range(RING)])  25.8 us
    all_to_all x1, blocking collectives, among_chips(): return lax.all_to_all(x, ('x', 'y'), 0, 0, tiled=True)  24.6 us
    pallas_call x11, Pallas kernels, local_call(): pl.pallas_call(body, out_shape=out_shape, grid=(1,) if fetch else (), in_...  15.4 us
    ppermute x3, waiting for transfers between devices, along_x(): return lax.ppermute(x, 'x', [(i, (i + by) % XS) for i in range(XS)])  14.2 us
    ppermute x3, starting transfers between devices, core_swap(): return lax.ppermute(x, 'core', [(0, 1), (1, 0)])  11.3 us
    ppermute x1, waiting for transfers between devices, on_device(): arrived = (stay, lax.ppermute(leave, 'y', [(0, 1), (1, 0)]))  3.78 us
  transfers between devices with their start and end apart: 36, of which 19 were waited for; matrix products, arithmetic and copies ran while one was open for 2% of the time, Pallas kernels for 8%

commit v1 on v0

--- a/solution.py
+++ b/solution.py
@@ -31,6 +31,10 @@
 
 def among_chips(x):
     return lax.all_to_all(x, ("x", "y"), 0, 0, tiled=True)
+
+
+def along_y(x):
+    return lax.ppermute(x, "y", [(0, 1), (1, 0)])
 
 
 def along_x(x, by):
@@ -158,13 +162,14 @@
         give_ref[:, cols] = jnp.where(dp == 0, halves[1], halves[0]).astype(BF16)
 
 
-def pair_body(deltas, where_ref, keep_ref, got_ref, keep_last_ref, got_last_ref, out_ref):
-    here, x = where_ref[0], where_ref[2]
+def pair_body(deltas, where_ref, keep_ref, keep_last_ref, got_ref, out_ref):
+    here, x, y = where_ref[0], where_ref[2], where_ref[3]
     size = out_ref.shape[2]
 
     def place(delta):
         chip = lax.rem(here + delta, RING)
-        return lax.rem(lax.div(chip, YS) - x + XS, XS), lax.rem(chip, YS)
+        along = lax.rem(lax.div(chip, YS) - x + XS, XS)
+        return lax.rem(lax.rem(chip, YS) + y, YS), along
 
     for n, delta in enumerate(deltas):
         rows = slice(n * size, (n + 1) * size)
@@ -172,21 +177,24 @@
             keep_ref[rows] + got_ref[rows].astype(F32)
         ).astype(BF16)
     out_ref[place(RING // 2)] = (
-        keep_last_ref[...] + got_last_ref[...].astype(F32)
+        keep_last_ref[...] + got_ref[len(deltas) * size :].astype(F32)
     ).astype(BF16)
 
 
-def column_body(y_ref, *refs):
-    y = y_ref[0]
-    stay_ref, leave_ref = refs[-2:]
-    stay = sum(ref[y].astype(F32) for ref in refs[:-2])
-    leave = sum(ref[1 - y].astype(F32) for ref in refs[:-2])
-    stay_ref[...] = stay
-    leave_ref[...] = leave.astype(BF16)
-
-
-def scatter_body(count_ref, stay_ref, got_ref, index_ref, gate_ref, mixed_ref, grad_ref):
-    total = stay_ref[...] + got_ref[...].astype(F32)
+def add(refs):
+    total = refs[0][...].astype(F32)
+    for ref in refs[1:]:
+        total = total + ref[...].astype(F32)
+    return total
+
+
+def leave_body(where_ref, *refs):
+    refs[-1][...] = add(refs[:-1]).astype(BF16)
+
+
+def scatter_body(count_ref, *refs):
+    index_ref, gate_ref, mixed_ref, grad_ref = refs[-4:]
+    total = add(refs[:-4])
     token_count, width = mixed_ref.shape
     place, weight, live = routes(count_ref, index_ref, gate_ref, token_count)
     out_rows = (weight * total[:, :width]).astype(BF16)
@@ -203,7 +211,7 @@
     block = gate_weight.shape[0]
     units = 3 * block
     here = lax.axis_index("tensor")
-    where = jnp.stack([here, lax.axis_index("dp"), lax.axis_index("x")]).astype(jnp.int32)
+    where = jnp.stack([here, lax.axis_index("dp"), lax.axis_index("x"), lax.axis_index("y")]).astype(jnp.int32)
     routing = [route_index[None, :], route_gate[None, :]]
 
     w_rows = jnp.concatenate(
@@ -300,7 +308,7 @@
         )
         kept.append(keep)
         given.append(give)
-    swapped = [core_swap(give) for give in lax.optimization_barrier(given)]
+    swapped = core_swap(jnp.concatenate(given, axis=0))
 
     part = width // 2
     pieces = [halves[delta][h] for deltas in (first, rest) for h in range(2) for delta in deltas]
@@ -316,20 +324,19 @@
     by_chip = local_call(
         functools.partial(pair_body, near),
         "pair_sum",
-        jax.ShapeDtypeStruct((XS, YS, capacity, 2 * width), BF16),
-        [where, kept[0], swapped[0], kept[1], swapped[1]],
-    )
-    along = [by_chip[0]] + [along_x(by_chip[by], by) for by in (1, 3, 2)]
-    stay, leave = local_call(
-        column_body,
-        "x_sum",
-        [
-            jax.ShapeDtypeStruct((capacity, 2 * width), F32),
-            jax.ShapeDtypeStruct((capacity, 2 * width), BF16),
-        ],
-        [lax.axis_index("y")[None].astype(jnp.int32)] + along,
-    )
-    arrived = (stay, lax.ppermute(leave, "y", [(0, 1), (1, 0)]))
+        jax.ShapeDtypeStruct((YS, XS, capacity, 2 * width), BF16),
+        [where, kept[0], kept[1], swapped],
+    )
+    across = along_x(by_chip[:, 2], 2)
+    leave = [across[1]] + [along_x(by_chip[1, by], by) for by in (1, 3)]
+    stay = [across[0]] + [along_x(by_chip[0, by], by) for by in (1, 3)]
+    gone = local_call(
+        leave_body,
+        "leave_sum",
+        jax.ShapeDtypeStruct((capacity, 2 * width), BF16),
+        [where, by_chip[1, 0]] + leave,
+    )
+    arrived = [by_chip[0, 0]] + stay + [along_y(gone)]
     mixed, input_grad = local_call(
         scatter_body,
         "scatter_rows",

time: 140 us -> 136 us (0.971)
  waiting for transfers between devices: 43.8 us -> 37.5 us
  starting transfers between devices: 51.4 us -> 53.6 us
    ppermute x3 -> x5, waiting for transfers between devices: 14.2 us -> 7.31 us  [along_x(): return lax.ppermute(x, 'x', [(i, (i + by) % XS) for i in range(XS)])]
    ppermute x3 -> x5, starting transfers between devices: 2.75 us -> 5.89 us  [along_x(): return lax.ppermute(x, 'x', [(i, (i + by) % XS) for i in range(XS)])]
    ppermute x3 -> x2, starting transfers between devices: 11.3 us -> 11.2 us  [core_swap(): return lax.ppermute(x, 'core', [(0, 1), (1, 0)])]
  transfers between devices with their start and end apart: 36 -> 37, of which waited for: 19 -> 19; matrix products, arithmetic and copies ran while one was open for 2% -> 2% of each run, Pallas kernels for 8% -> 8%
where the time goes in v1:
time: 136 us
  starting transfers between devices  53.6 us (39%)
  waiting for transfers between devices  37.5 us (28%)
  blocking collectives  24.6 us (18%)
  Pallas kernels  15.9 us (12%)
  between operations  1.62 us (1%)
  other arithmetic  1.59 us (1%)
    ppermute x28, starting transfers between devices, ring(): lax.ppermute(x, 'tensor', [(z, (z + by) % RING) for z in range(RING)])  35.2 us
    ppermute x28, waiting for transfers between devices, ring(): lax.ppermute(x, 'tensor', [(z, (z + by) % RING) for z in range(RING)])  25.9 us
    all_to_all x1, blocking collectives, among_chips(): return lax.all_to_all(x, ('x', 'y'), 0, 0, tiled=True)  24.6 us
    pallas_call x11, Pallas kernels, local_call(): pl.pallas_call(body, out_shape=out_shape, grid=(1,) if fetch else (), in_...  15.9 us
    ppermute x2, starting transfers between devices, core_swap(): return lax.ppermute(x, 'core', [(0, 1), (1, 0)])  11.2 us
    ppermute x5, waiting for transfers between devices, along_x(): return lax.ppermute(x, 'x', [(i, (i + by) % XS) for i in range(XS)])  7.31 us
    ppermute x5, starting transfers between devices, along_x(): return lax.ppermute(x, 'x', [(i, (i + by) % XS) for i in range(XS)])  5.89 us
    ppermute x1, waiting for transfers between devices, along_y(): return lax.ppermute(x, 'y', [(0, 1), (1, 0)])  4.35 us
  transfers between devices with their start and end apart: 37, of which 19 were waited for; matrix products, arithmetic and copies ran while one was open for 2% of the time, Pallas kernels for 8%

profile of v1, /device:TPU:1, one launch (start us, length us, event | category | flops | bytes accessed | tf_op | source)
XLA Modules:
  0.0 136.2 jit_solution(15297776552697353265)
XLA Ops:
  1.3 2.4 %gather_rows.1 = bf16[8,96,768]{2,1,0:T(8,128)(2,1)} custom-call(s32[1]{0:T(128)S(6)} %copy.15.count_ref, bf16[256,384]{1,0:T(8,128)(2,1)} %tokens_ref.1, bf16[256,384]{1,0:T(8,128)(2,1)} %grads_ref.1, s32[1,96]{1,0:T(1,128)} %bitcast.32, f32[1,96]{1,0:T(1,128)} %bitcast.34), custom_call_target="tpu_custom_call" | custom-call | flops 1 | bytes 1 | tf_op jit(solution)/shard_map/gather_rows/pallas_call | solution.py:53
  3.7 24.6 %all_to_all.5.rows_ref = bf16[8,96,768]{2,1,0:T(8,128)(2,1)S(1)} all-to-all(bf16[8,96,768]{2,1,0:T(8,128)(2,1)} %gather_rows.1), channel_id=1, replica_groups=mesh['x'=4,'y'=2,'core'=2,'tensor'=8,'dp'=2] {'x','y'}, dimensions={0} | all-to-all | bytes 2359296 | tf_op jit(solution)/shard_map/all_to_all | solution.py:33
  28.3 2.4 %collective-permute-start = (bf16[8,96,768]{2,1,0:T(8,128)(2,1)S(1)}, bf16[8,96,768]{2,1,0:T(8,128)(2,1)S(1)}, u32[]{:S(2)}, u32[]{:S(2)}) collective-permute-start(bf16[8,96,768]{2,1,0:T(8,128)(2,1)S(1)} %all_to_all.5.rows_ref), channel_id=1, source_target_pairs={{0,16},{16,0},{1,17},{17,1},{2,18},{18,2},{3,19},{19,3},{4,20},{20... | collective-permute-start | bytes 3538952 | tf_op jit(solution)/shard_map/ppermute | solution.py:29
  32.2 5.7 %collective-permute-start.1 = (bf16[96,1008]{1,0:T(8,128)(2,1)S(1)}, bf16[96,1008]{1,0:T(8,128)(2,1)S(1)}, u32[]{:S(2)}, u32[]{:S(2)}) collective-permute-start(bf16[96,1008]{1,0:T(8,128)(2,1)S(1)} %get-tuple-element.46), channel_id=1, source_target_pairs={{0,14},{2,0},{4,2},{6,4},{8,6},{10,8},{12,10},{14,12},{1,15},{3,1}... | collective-permute-start | bytes 580616 | tf_op jit(solution)/shard_map/ppermute | solution.py:45
  39.0 2.7 %collective-permute-start.14 = (bf16[96,1008]{1,0:T(8,128)(2,1)S(1)}, bf16[96,1008]{1,0:T(8,128)(2,1)S(1)}, u32[]{:S(2)}, u32[]{:S(2)}) collective-permute-start(bf16[96,1008]{1,0:T(8,128)(2,1)S(1)} %get-tuple-element.56), channel_id=1, source_target_pairs={{0,14},{2,0},{4,2},{6,4},{8,6},{10,8},{12,10},{14,12},{1,15},{3,1}... | collective-permute-start | bytes 580616 | tf_op jit(solution)/shard_map/ppermute | solution.py:45
  42.2 3.1 %collective-permute-done.2 = bf16[96,1008]{1,0:T(8,128)(2,1)S(1)} collective-permute-done((bf16[96,1008]{1,0:T(8,128)(2,1)S(1)}, bf16[96,1008]{1,0:T(8,128)(2,1)S(1)}, u32[]{:S(2)}, u32[]{:S(2)}) %collective-permute-start.2) | collective-permute-done | bytes 193568 | tf_op jit(solution)/shard_map/ppermute | solution.py:45
  50.5 3.0 %collective-permute-start.4 = (bf16[96,1008]{1,0:T(8,128)(2,1)S(1)}, bf16[96,1008]{1,0:T(8,128)(2,1)S(1)}, u32[]{:S(2)}, u32[]{:S(2)}) collective-permute-start(bf16[96,1008]{1,0:T(8,128)(2,1)S(1)} %add_convert_fusion.8), channel_id=1, source_target_pairs={{0,14},{2,0},{4,2},{6,4},{8,6},{10,8},{12,10},{14,12},{1,15},{3,1}... | collective-permute-start | bytes 580616 | tf_op jit(solution)/shard_map/ppermute | solution.py:45
  53.8 2.7 %collective-permute-start.15 = (bf16[96,1008]{1,0:T(8,128)(2,1)S(1)}, bf16[96,1008]{1,0:T(8,128)(2,1)S(1)}, u32[]{:S(2)}, u32[]{:S(2)}) collective-permute-start(bf16[96,1008]{1,0:T(8,128)(2,1)S(1)} %add_convert_fusion.4), channel_id=1, source_target_pairs={{0,14},{2,0},{4,2},{6,4},{8,6},{10,8},{12,10},{14,12},{1,15},{3,1}... | collective-permute-start | bytes 580616 | tf_op jit(solution)/shard_map/ppermute | solution.py:45
  56.5 3.5 %collective-permute-start.5 = (bf16[96,1008]{1,0:T(8,128)(2,1)S(1)}, bf16[96,1008]{1,0:T(8,128)(2,1)S(1)}, u32[]{:S(2)}, u32[]{:S(2)}) collective-permute-start(bf16[96,1008]{1,0:T(8,128)(2,1)S(1)} %add_convert_fusion.7), channel_id=1, source_target_pairs={{0,14},{2,0},{4,2},{6,4},{8,6},{10,8},{12,10},{14,12},{1,15},{3,1}... | collective-permute-start | bytes 580616 | tf_op jit(solution)/shard_map/ppermute | solution.py:45
  60.4 3.2 %collective-permute-start.16 = (bf16[96,1008]{1,0:T(8,128)(2,1)S(1)}, bf16[96,1008]{1,0:T(8,128)(2,1)S(1)}, u32[]{:S(2)}, u32[]{:S(2)}) collective-permute-start(bf16[96,1008]{1,0:T(8,128)(2,1)S(1)} %add_convert_fusion.3), channel_id=1, source_target_pairs={{0,14},{2,0},{4,2},{6,4},{8,6},{10,8},{12,10},{14,12},{1,15},{3,1}... | collective-permute-start | bytes 580616 | tf_op jit(solution)/shard_map/ppermute | solution.py:45
  63.6 2.3 %collective-permute-done.19 = bf16[96,1008]{1,0:T(8,128)(2,1)S(1)} collective-permute-done((bf16[96,1008]{1,0:T(8,128)(2,1)S(1)}, bf16[96,1008]{1,0:T(8,128)(2,1)S(1)}, u32[]{:S(2)}, u32[]{:S(2)}) %collective-permute-start.19) | collective-permute-done | bytes 193568 | tf_op jit(solution)/shard_map/ppermute | solution.py:45
  68.4 3.9 %collective-permute-done.20 = bf16[96,1008]{1,0:T(8,128)(2,1)S(1)} collective-permute-done((bf16[96,1008]{1,0:T(8,128)(2,1)S(1)}, bf16[96,1008]{1,0:T(8,128)(2,1)S(1)}, u32[]{:S(2)}, u32[]{:S(2)}) %collective-permute-start.20) | collective-permute-done | bytes 193568 | tf_op jit(solution)/shard_map/ppermute | solution.py:45
  81.1 2.9 %collective-permute-done.10.refs_3_.refs_11_ = bf16[96,1008]{1,0:T(8,128)(2,1)S(1)} collective-permute-done((bf16[96,1008]{1,0:T(8,128)(2,1)S(1)}, bf16[96,1008]{1,0:T(8,128)(2,1)S(1)}, u32[]{:S(2)}, u32[]{:S(2)}) %collective-permute-start.10) | collective-permute-done | bytes 193568 | tf_op jit(solution)/shard_map/ppermute | solution.py:45
  84.1 2.7 %collective-permute-start.26 = (bf16[96,1008]{1,0:T(8,128)(2,1)S(1)}, bf16[96,1008]{1,0:T(8,128)(2,1)S(1)}, u32[]{:S(2)}, u32[]{:S(2)}) collective-permute-start(bf16[96,1008]{1,0:T(8,128)(2,1)S(1)} %collective-permute-done.24.refs_11_.refs_15_), channel_id=1, source_target_pairs={{0,14},{2,0},{4,2},{6,4},{8,6},{10,8},{12,10},{14,12},{1,15},{3,1}... | collective-permute-start | bytes 580616 | tf_op jit(solution)/shard_map/ppermute | solution.py:45
  86.8 2.2 %collective-permute-start.13 = (bf16[96,1008]{1,0:T(8,128)(2,1)S(1)}, bf16[96,1008]{1,0:T(8,128)(2,1)S(1)}, u32[]{:S(2)}, u32[]{:S(2)}) collective-permute-start(bf16[96,1008]{1,0:T(8,128)(2,1)S(1)} %collective-permute-done.11.refs_4_.refs_10_), channel_id=1, source_target_pairs={{0,14},{2,0},{4,2},{6,4},{8,6},{10,8},{12,10},{14,12},{1,15},{3,1}... | collective-permute-start | bytes 580616 | tf_op jit(solution)/shard_map/ppermute | solution.py:45
  89.2 3.6 %collective-permute-done.12.refs_5_.refs_6_ = bf16[96,1008]{1,0:T(8,128)(2,1)S(1)} collective-permute-done((bf16[96,1008]{1,0:T(8,128)(2,1)S(1)}, bf16[96,1008]{1,0:T(8,128)(2,1)S(1)}, u32[]{:S(2)}, u32[]{:S(2)}) %collective-permute-start.12) | collective-permute-done | bytes 193568 | tf_op jit(solution)/shard_map/ppermute | solution.py:45
  92.8 2.7 %collective-permute-start.28 = (bf16[96,1008]{1,0:T(8,128)(2,1)S(1)}, bf16[96,1008]{1,0:T(8,128)(2,1)S(1)}, u32[]{:S(2)}, u32[]{:S(2)}) collective-permute-start(bf16[96,1008]{1,0:T(8,128)(2,1)S(1)} %collective-permute-done.26.refs_13_.refs_8_), channel_id=1, source_target_pairs={{0,14},{2,0},{4,2},{6,4},{8,6},{10,8},{12,10},{14,12},{1,15},{3,1}... | collective-permute-start | bytes 580616 | tf_op jit(solution)/shard_map/ppermute | solution.py:45
  95.5 2.4 %out_near.1 = (f32[672,768]{1,0:T(8,128)S(1)}, bf16[672,768]{1,0:T(8,128)(2,1)S(1)}) custom-call(s32[4]{0:T(128)S(1)} %pad_add_fusion.where_ref, bf16[768,384]{1,0:T(8,128)(2,1)S(1)} %maximum_maximum_fusion.w_rows_ref, bf16[368,384]{1,0:T(8,128)(2,1)S(1)} %concatenate.16.w_grads_ref, bf16[96,1008]{1,0:T(8,128)(2,1)S(1)} %pad_maximum_fusion.1.refs_0_.refs_14_, ...), custom_call_target="tpu_custom_call" | custom-call | flops 1 | bytes 1 | tf_op jit(solution)/shard_map/out_near/pallas_call | solution.py:53
  97.9 3.0 %collective-permute-done.27.refs_0_.refs_4_ = bf16[96,1008]{1,0:T(8,128)(2,1)S(1)} collective-permute-done((bf16[96,1008]{1,0:T(8,128)(2,1)S(1)}, bf16[96,1008]{1,0:T(8,128)(2,1)S(1)}, u32[]{:S(2)}, u32[]{:S(2)}) %collective-permute-start.27) | collective-permute-done | bytes 193568 | tf_op jit(solution)/shard_map/ppermute | solution.py:45
  101.9 8.8 %collective-permute-start.29 = (bf16[768,768]{1,0:T(8,128)(2,1)S(1)}, bf16[768,768]{1,0:T(8,128)(2,1)S(1)}, u32[]{:S(2)}, u32[]{:S(2)}) collective-permute-start(bf16[768,768]{1,0:T(8,128)(2,1)S(1)} %pad_maximum_fusion), channel_id=1, source_target_pairs={{0,16},{16,0},{1,17},{17,1},{2,18},{18,2},{3,19},{19,3},{4,20},{20... | collective-permute-start | bytes 3538952 | tf_op jit(solution)/shard_map/ppermute | solution.py:29
  110.7 2.8 %weight_grads.1 = (f32[192,1008]{1,0:T(8,128)S(1)}, bf16[192,1008]{1,0:T(8,128)(2,1)S(1)}) custom-call(s32[4]{0:T(128)S(1)} %pad_add_fusion.where_ref, bf16[288,768]{1,0:T(8,128)(2,1)S(1)} %get-tuple-element.65.refs_0_, bf16[288,768]{1,0:T(8,128)(2,1)S(1)} %get-tuple-element.66.refs_1_, bf16[480,768]{1,0:T(8,128)(2,1)S(1)} %get-tuple-element.67.refs_2_, ...), custom_call_target="tpu_custom_call" | custom-call | flops 1 | bytes 1 | tf_op jit(solution)/shard_map/weight_grads/pallas_call | solution.py:53
  117.7 2.6 %collective-permute-start.32 = (bf16[96,768]{1,0:T(8,128)(2,1)S(1)}, bf16[96,768]{1,0:T(8,128)(2,1)S(1)}, u32[]{:S(2)}, u32[]{:S(2)}) collective-permute-start(bf16[96,768]{1,0:T(8,128)(2,1)S(1)} %get-tuple-element.78), channel_id=1, source_target_pairs={{0,192},{64,0},{128,64},{192,128},{1,193},{65,1},{129,65},{193,129... | collective-permute-start | bytes 442376 | tf_op jit(solution)/shard_map/ppermute | solution.py:41
  120.4 4.2 %collective-permute-done.30 = bf16[2,96,768]{2,1,0:T(8,128)(2,1)S(1)} collective-permute-done((bf16[2,96,768]{2,1,0:T(8,128)(2,1)S(1)}, bf16[2,96,768]{2,1,0:T(8,128)(2,1)S(1)}, u32[]{:S(2)}, u32[]{:S(2)}) %collective-permute-start.30) | collective-permute-done | bytes 294944 | tf_op jit(solution)/shard_map/ppermute | solution.py:41
  130.8 4.4 %collective-permute-done.35.refs_4_ = bf16[96,768]{1,0:T(8,128)(2,1)S(1)} collective-permute-done((bf16[96,768]{1,0:T(8,128)(2,1)S(1)}, bf16[96,768]{1,0:T(8,128)(2,1)S(1)}, u32[]{:S(2)}, u32[]{:S(2)}) %collective-permute-start.35) | collective-permute-done | bytes 147488 | tf_op jit(solution)/shard_map/ppermute | solution.py:37
  (99 shorter events, 32.7 us)
Async XLA Ops:
  28.3 9.6 %collective-permute-start = (bf16[8,96,768]{2,1,0:T(8,128)(2,1)S(1)}, bf16[8,96,768]{2,1,0:T(8,128)(2,1)S(1)}, u32[]{:S(2)}, u32[]{:S(2)}) collective-permute-start(bf16[8,96,768]{2,1,0:T(8,128)(2,1)S(1)} %all_to_all.5.rows_ref), channel_id=1, source_target_pairs={{0,16},{16,0},{1,17},{17,1},{2,18},{18,2},{3,19},{19,3},{4,20},{20... | collective-permute-start | bytes 3538952 | tf_op jit(solution)/shard_map/ppermute | solution.py:29
  32.2 10.0 %collective-permute-start.1 = (bf16[96,1008]{1,0:T(8,128)(2,1)S(1)}, bf16[96,1008]{1,0:T(8,128)(2,1)S(1)}, u32[]{:S(2)}, u32[]{:S(2)}) collective-permute-start(bf16[96,1008]{1,0:T(8,128)(2,1)S(1)} %get-tuple-element.46), channel_id=1, source_target_pairs={{0,14},{2,0},{4,2},{6,4},{8,6},{10,8},{12,10},{14,12},{1,15},{3,1}... | collective-permute-start | bytes 580616 | tf_op jit(solution)/shard_map/ppermute | solution.py:45
  37.9 7.4 %collective-permute-start.2 = (bf16[96,1008]{1,0:T(8,128)(2,1)S(1)}, bf16[96,1008]{1,0:T(8,128)(2,1)S(1)}, u32[]{:S(2)}, u32[]{:S(2)}) collective-permute-start(bf16[96,1008]{1,0:T(8,128)(2,1)S(1)} %get-tuple-element.47), channel_id=1, source_target_pairs={{0,2},{2,4},{4,6},{6,8},{8,10},{10,12},{12,14},{14,0},{1,3},{3,5},... | collective-permute-start | bytes 580616 | tf_op jit(solution)/shard_map/ppermute | solution.py:45
  39.0 14.7 %collective-permute-start.14 = (bf16[96,1008]{1,0:T(8,128)(2,1)S(1)}, bf16[96,1008]{1,0:T(8,128)(2,1)S(1)}, u32[]{:S(2)}, u32[]{:S(2)}) collective-permute-start(bf16[96,1008]{1,0:T(8,128)(2,1)S(1)} %get-tuple-element.56), channel_id=1, source_target_pairs={{0,14},{2,0},{4,2},{6,4},{8,6},{10,8},{12,10},{14,12},{1,15},{3,1}... | collective-permute-start | bytes 580616 | tf_op jit(solution)/shard_map/ppermute | solution.py:45
  41.8 8.0 %collective-permute-start.17 = (bf16[96,1008]{1,0:T(8,128)(2,1)S(1)}, bf16[96,1008]{1,0:T(8,128)(2,1)S(1)}, u32[]{:S(2)}, u32[]{:S(2)}) collective-permute-start(bf16[96,1008]{1,0:T(8,128)(2,1)S(1)} %get-tuple-element.60), channel_id=1, source_target_pairs={{0,2},{2,4},{4,6},{6,8},{8,10},{10,12},{12,14},{14,0},{1,3},{3,5},... | collective-permute-start | bytes 580616 | tf_op jit(solution)/shard_map/ppermute | solution.py:45
  49.8 10.2 %collective-permute-start.18 = (bf16[96,1008]{1,0:T(8,128)(2,1)S(1)}, bf16[96,1008]{1,0:T(8,128)(2,1)S(1)}, u32[]{:S(2)}, u32[]{:S(2)}) collective-permute-start(bf16[96,1008]{1,0:T(8,128)(2,1)S(1)} %add_convert_fusion.2), channel_id=1, source_target_pairs={{0,2},{2,4},{4,6},{6,8},{8,10},{10,12},{12,14},{14,0},{1,3},{3,5},... | collective-permute-start | bytes 580616 | tf_op jit(solution)/shard_map/ppermute | solution.py:45
  53.6 12.4 %collective-permute-start.7 = (bf16[96,1008]{1,0:T(8,128)(2,1)S(1)}, bf16[96,1008]{1,0:T(8,128)(2,1)S(1)}, u32[]{:S(2)}, u32[]{:S(2)}) collective-permute-start(bf16[96,1008]{1,0:T(8,128)(2,1)S(1)} %add_convert_fusion.5), channel_id=1, source_target_pairs={{0,2},{2,4},{4,6},{6,8},{8,10},{10,12},{12,14},{14,0},{1,3},{3,5},... | collective-permute-start | bytes 580616 | tf_op jit(solution)/shard_map/ppermute | solution.py:45
  56.5 9.5 %collective-permute-start.5 = (bf16[96,1008]{1,0:T(8,128)(2,1)S(1)}, bf16[96,1008]{1,0:T(8,128)(2,1)S(1)}, u32[]{:S(2)}, u32[]{:S(2)}) collective-permute-start(bf16[96,1008]{1,0:T(8,128)(2,1)S(1)} %add_convert_fusion.7), channel_id=1, source_target_pairs={{0,14},{2,0},{4,2},{6,4},{8,6},{10,8},{12,10},{14,12},{1,15},{3,1}... | collective-permute-start | bytes 580616 | tf_op jit(solution)/shard_map/ppermute | solution.py:45
  60.4 8.0 %collective-permute-start.16 = (bf16[96,1008]{1,0:T(8,128)(2,1)S(1)}, bf16[96,1008]{1,0:T(8,128)(2,1)S(1)}, u32[]{:S(2)}, u32[]{:S(2)}) collective-permute-start(bf16[96,1008]{1,0:T(8,128)(2,1)S(1)} %add_convert_fusion.3), channel_id=1, source_target_pairs={{0,14},{2,0},{4,2},{6,4},{8,6},{10,8},{12,10},{14,12},{1,15},{3,1}... | collective-permute-start | bytes 580616 | tf_op jit(solution)/shard_map/ppermute | solution.py:45
  66.4 8.0 %collective-permute-start.8 = (bf16[96,1008]{1,0:T(8,128)(2,1)S(1)}, bf16[96,1008]{1,0:T(8,128)(2,1)S(1)}, u32[]{:S(2)}, u32[]{:S(2)}) collective-permute-start(bf16[96,1008]{1,0:T(8,128)(2,1)S(1)} %pad_maximum_fusion.1.refs_0_.refs_14_), channel_id=1, source_target_pairs={{0,2},{2,4},{4,6},{6,8},{8,10},{10,12},{12,14},{14,0},{1,3},{3,5},... | collective-permute-start | bytes 580616 | tf_op jit(solution)/shard_map/ppermute | solution.py:45
  72.9 8.2 %collective-permute-start.21 = (bf16[96,1008]{1,0:T(8,128)(2,1)S(1)}, bf16[96,1008]{1,0:T(8,128)(2,1)S(1)}, u32[]{:S(2)}, u32[]{:S(2)}) collective-permute-start(bf16[96,1008]{1,0:T(8,128)(2,1)S(1)} %pad_maximum_fusion.2.refs_7_.refs_19_), channel_id=1, source_target_pairs={{0,2},{2,4},{4,6},{6,8},{8,10},{10,12},{12,14},{14,0},{1,3},{3,5},... | collective-permute-start | bytes 580616 | tf_op jit(solution)/shard_map/ppermute | solution.py:45
  74.4 9.6 %collective-permute-start.10 = (bf16[96,1008]{1,0:T(8,128)(2,1)S(1)}, bf16[96,1008]{1,0:T(8,128)(2,1)S(1)}, u32[]{:S(2)}, u32[]{:S(2)}) collective-permute-start(bf16[96,1008]{1,0:T(8,128)(2,1)S(1)} %collective-permute-done.8.refs_1_.refs_13_), channel_id=1, source_target_pairs={{0,2},{2,4},{4,6},{6,8},{8,10},{10,12},{12,14},{14,0},{1,3},{3,5},... | collective-permute-start | bytes 580616 | tf_op jit(solution)/shard_map/ppermute | solution.py:45
  81.0 8.1 %collective-permute-start.23 = (bf16[96,1008]{1,0:T(8,128)(2,1)S(1)}, bf16[96,1008]{1,0:T(8,128)(2,1)S(1)}, u32[]{:S(2)}, u32[]{:S(2)}) collective-permute-start(bf16[96,1008]{1,0:T(8,128)(2,1)S(1)} %collective-permute-done.21.refs_8_.refs_18_), channel_id=1, source_target_pairs={{0,2},{2,4},{4,6},{6,8},{8,10},{10,12},{12,14},{14,0},{1,3},{3,5},... | collective-permute-start | bytes 580616 | tf_op jit(solution)/shard_map/ppermute | solution.py:45
  84.1 8.7 %collective-permute-start.12 = (bf16[96,1008]{1,0:T(8,128)(2,1)S(1)}, bf16[96,1008]{1,0:T(8,128)(2,1)S(1)}, u32[]{:S(2)}, u32[]{:S(2)}) collective-permute-start(bf16[96,1008]{1,0:T(8,128)(2,1)S(1)} %collective-permute-done.10.refs_3_.refs_11_), channel_id=1, source_target_pairs={{0,2},{2,4},{4,6},{6,8},{8,10},{10,12},{12,14},{14,0},{1,3},{3,5},... | collective-permute-start | bytes 580616 | tf_op jit(solution)/shard_map/ppermute | solution.py:45
  84.1 8.7 %collective-permute-start.26 = (bf16[96,1008]{1,0:T(8,128)(2,1)S(1)}, bf16[96,1008]{1,0:T(8,128)(2,1)S(1)}, u32[]{:S(2)}, u32[]{:S(2)}) collective-permute-start(bf16[96,1008]{1,0:T(8,128)(2,1)S(1)} %collective-permute-done.24.refs_11_.refs_15_), channel_id=1, source_target_pairs={{0,14},{2,0},{4,2},{6,4},{8,6},{10,8},{12,10},{14,12},{1,15},{3,1}... | collective-permute-start | bytes 580616 | tf_op jit(solution)/shard_map/ppermute | solution.py:45
  86.8 8.7 %collective-permute-start.13 = (bf16[96,1008]{1,0:T(8,128)(2,1)S(1)}, bf16[96,1008]{1,0:T(8,128)(2,1)S(1)}, u32[]{:S(2)}, u32[]{:S(2)}) collective-permute-start(bf16[96,1008]{1,0:T(8,128)(2,1)S(1)} %collective-permute-done.11.refs_4_.refs_10_), channel_id=1, source_target_pairs={{0,14},{2,0},{4,2},{6,4},{8,6},{10,8},{12,10},{14,12},{1,15},{3,1}... | collective-permute-start | bytes 580616 | tf_op jit(solution)/shard_map/ppermute | solution.py:45
  92.8 8.1 %collective-permute-start.27 = (bf16[96,1008]{1,0:T(8,128)(2,1)S(1)}, bf16[96,1008]{1,0:T(8,128)(2,1)S(1)}, u32[]{:S(2)}, u32[]{:S(2)}) collective-permute-start(bf16[96,1008]{1,0:T(8,128)(2,1)S(1)} %collective-permute-done.12.refs_5_.refs_6_), channel_id=1, source_target_pairs={{0,2},{2,4},{4,6},{6,8},{8,10},{10,12},{12,14},{14,0},{1,3},{3,5},... | collective-permute-start | bytes 580616 | tf_op jit(solution)/shard_map/ppermute | solution.py:45
  92.8 8.1 %collective-permute-start.28 = (bf16[96,1008]{1,0:T(8,128)(2,1)S(1)}, bf16[96,1008]{1,0:T(8,128)(2,1)S(1)}, u32[]{:S(2)}, u32[]{:S(2)}) collective-permute-start(bf16[96,1008]{1,0:T(8,128)(2,1)S(1)} %collective-permute-done.26.refs_13_.refs_8_), channel_id=1, source_target_pairs={{0,14},{2,0},{4,2},{6,4},{8,6},{10,8},{12,10},{14,12},{1,15},{3,1}... | collective-permute-start | bytes 580616 | tf_op jit(solution)/shard_map/ppermute | solution.py:45
  101.9 11.6 %collective-permute-start.29 = (bf16[768,768]{1,0:T(8,128)(2,1)S(1)}, bf16[768,768]{1,0:T(8,128)(2,1)S(1)}, u32[]{:S(2)}, u32[]{:S(2)}) collective-permute-start(bf16[768,768]{1,0:T(8,128)(2,1)S(1)} %pad_maximum_fusion), channel_id=1, source_target_pairs={{0,16},{16,0},{1,17},{17,1},{2,18},{18,2},{3,19},{19,3},{4,20},{20... | collective-permute-start | bytes 3538952 | tf_op jit(solution)/shard_map/ppermute | solution.py:29
  114.3 10.2 %collective-permute-start.30 = (bf16[2,96,768]{2,1,0:T(8,128)(2,1)S(1)}, bf16[2,96,768]{2,1,0:T(8,128)(2,1)S(1)}, u32[]{:S(2)}, u32[]{:S(2)}) collective-permute-start(bf16[2,96,768]{2,1,0:T(8,128)(2,1)S(1)} %slice_bitcast_fusion.3), channel_id=1, source_target_pairs={{0,128},{64,192},{128,0},{192,64},{1,129},{65,193},{129,1},{193,65... | collective-permute-start | bytes 884744 | tf_op jit(solution)/shard_map/ppermute | solution.py:41
  115.7 13.8 %collective-permute-start.36 = (bf16[192,1008]{1,0:T(8,128)(2,1)S(1)}, bf16[192,1008]{1,0:T(8,128)(2,1)S(1)}, u32[]{:S(2)}, u32[]{:S(2)}) collective-permute-start(bf16[192,1008]{1,0:T(8,128)(2,1)S(1)} %get-tuple-element.74), channel_id=1, source_target_pairs={{0,1},{1,0},{2,3},{3,2},{4,5},{5,4},{6,7},{7,6},{8,9},{9,8},{10,11... | collective-permute-start | bytes 1161224 | tf_op jit(solution)/shard_map/ppermute | solution.py:323
  116.2 10.1 %collective-permute-start.34 = (bf16[96,768]{1,0:T(8,128)(2,1)S(1)}, bf16[96,768]{1,0:T(8,128)(2,1)S(1)}, u32[]{:S(2)}, u32[]{:S(2)}) collective-permute-start(bf16[96,768]{1,0:T(8,128)(2,1)S(1)} %get-tuple-element.75), channel_id=1, source_target_pairs={{0,192},{64,0},{128,64},{192,128},{1,193},{65,1},{129,65},{193,129... | collective-permute-start | bytes 442376 | tf_op jit(solution)/shard_map/ppermute | solution.py:41
  117.7 10.3 %collective-permute-start.33 = (bf16[96,768]{1,0:T(8,128)(2,1)S(1)}, bf16[96,768]{1,0:T(8,128)(2,1)S(1)}, u32[]{:S(2)}, u32[]{:S(2)}) collective-permute-start(bf16[96,768]{1,0:T(8,128)(2,1)S(1)} %get-tuple-element.76), channel_id=1, source_target_pairs={{0,64},{64,128},{128,192},{192,0},{1,65},{65,129},{129,193},{193,1... | collective-permute-start | bytes 442376 | tf_op jit(solution)/shard_map/ppermute | solution.py:41
  117.7 13.1 %collective-permute-start.32 = (bf16[96,768]{1,0:T(8,128)(2,1)S(1)}, bf16[96,768]{1,0:T(8,128)(2,1)S(1)}, u32[]{:S(2)}, u32[]{:S(2)}) collective-permute-start(bf16[96,768]{1,0:T(8,128)(2,1)S(1)} %get-tuple-element.78), channel_id=1, source_target_pairs={{0,192},{64,0},{128,64},{192,128},{1,193},{65,1},{129,65},{193,129... | collective-permute-start | bytes 442376 | tf_op jit(solution)/shard_map/ppermute | solution.py:41
  (18 other events, 173.5 us)

commit v2 on v1

--- a/solution.py
+++ b/solution.py
@@ -291,6 +291,10 @@
     for step in (1, 2, 3):
         right = [ring(a, 1) for a in right]
         left = [ring(a, -1) for a in left]
+        if step == 1:
+            right[0], left[0], acts_own[1] = lax.optimization_barrier(
+                (right[0], left[0], acts_own[1])
+            )
         halves[RING - step] = right
         halves[step] = left
     halves[4] = [ring(right[0], 1), ring(left[1], -1)]
@@ -337,20 +341,16 @@
         [where, by_chip[1, 0]] + leave,
     )
     arrived = [by_chip[0, 0]] + stay + [along_y(gone)]
+    grads_w = (keep_w + got_w.astype(F32)).T
+    grads = (grads_w[:block], grads_w[block : 2 * block], grads_w[2 * block :])
+    arrived[0], *grads = lax.optimization_barrier((arrived[0], *grads))
     mixed, input_grad = local_call(
         scatter_body,
         "scatter_rows",
         [jax.ShapeDtypeStruct((token_count, width), BF16)] * 2,
         [route_count, *arrived] + routing,
     )
-    grads_w = keep_w + got_w.astype(F32)
-    return (
-        mixed,
-        input_grad,
-        grads_w[:, :block].T,
-        grads_w[:, block : 2 * block].T,
-        grads_w[:, 2 * block :].T,
-    )
+    return (mixed, input_grad, *grads)
 
 
 def solution(mesh):

time: 136 us -> 136 us (level)
  waiting for transfers between devices: 37.5 us -> 40 us
  starting transfers between devices: 53.6 us -> 51.2 us
    ppermute x28, waiting for transfers between devices: 25.9 us -> 28.4 us  [ring(): lax.ppermute(x, 'tensor', [(z, (z + by) % RING) for z in range(RING)])]
    ppermute x28, starting transfers between devices: 35.2 us -> 33.2 us  [ring(): lax.ppermute(x, 'tensor', [(z, (z + by) % RING) for z in range(RING)])]
where the time goes in v2:
time: 136 us
  starting transfers between devices  51.2 us (38%)
  waiting for transfers between devices  40 us (29%)
  blocking collectives  24.6 us (18%)
  Pallas kernels  15.9 us (12%)
  between operations  1.61 us (1%)
  other arithmetic  1.55 us (1%)
    ppermute x28, starting transfers between devices, ring(): lax.ppermute(x, 'tensor', [(z, (z + by) % RING) for z in range(RING)])  33.2 us
    ppermute x28, waiting for transfers between devices, ring(): lax.ppermute(x, 'tensor', [(z, (z + by) % RING) for z in range(RING)])  28.4 us
    all_to_all x1, blocking collectives, among_chips(): return lax.all_to_all(x, ('x', 'y'), 0, 0, tiled=True)  24.6 us
    pallas_call x11, Pallas kernels, local_call(): pl.pallas_call(body, out_shape=out_shape, grid=(1,) if fetch else (), in_...  15.9 us
    ppermute x2, starting transfers between devices, core_swap(): return lax.ppermute(x, 'core', [(0, 1), (1, 0)])  10.7 us
    ppermute x5, waiting for transfers between devices, along_x(): return lax.ppermute(x, 'x', [(i, (i + by) % XS) for i in range(XS)])  7.3 us
    ppermute x5, starting transfers between devices, along_x(): return lax.ppermute(x, 'x', [(i, (i + by) % XS) for i in range(XS)])  5.9 us
    ppermute x1, waiting for transfers between devices, along_y(): return lax.ppermute(x, 'y', [(0, 1), (1, 0)])  4.34 us
  transfers between devices with their start and end apart: 37, of which 19 were waited for; matrix products, arithmetic and copies ran while one was open for 2% of the time, Pallas kernels for 8%

profile of v2, /device:TPU:1, one launch (start us, length us, event | category | flops | bytes accessed | tf_op | source)
XLA Modules:
  0.0 136.2 jit_solution(9576672548187341490)
XLA Ops:
  1.3 2.4 %gather_rows.1 = bf16[8,96,768]{2,1,0:T(8,128)(2,1)} custom-call(s32[1]{0:T(128)S(6)} %copy.15.count_ref, bf16[256,384]{1,0:T(8,128)(2,1)} %tokens_ref.1, bf16[256,384]{1,0:T(8,128)(2,1)} %grads_ref.1, s32[1,96]{1,0:T(1,128)} %bitcast.28, f32[1,96]{1,0:T(1,128)} %bitcast.30), custom_call_target="tpu_custom_call" | custom-call | flops 1 | bytes 1 | tf_op jit(solution)/shard_map/gather_rows/pallas_call | solution.py:53
  3.7 24.6 %all_to_all.5.rows_ref = bf16[8,96,768]{2,1,0:T(8,128)(2,1)S(1)} all-to-all(bf16[8,96,768]{2,1,0:T(8,128)(2,1)} %gather_rows.1), channel_id=1, replica_groups=mesh['x'=4,'y'=2,'core'=2,'tensor'=8,'dp'=2] {'x','y'}, dimensions={0} | all-to-all | bytes 2359296 | tf_op jit(solution)/shard_map/all_to_all | solution.py:33
  28.3 2.4 %collective-permute-start = (bf16[8,96,768]{2,1,0:T(8,128)(2,1)S(1)}, bf16[8,96,768]{2,1,0:T(8,128)(2,1)S(1)}, u32[]{:S(2)}, u32[]{:S(2)}) collective-permute-start(bf16[8,96,768]{2,1,0:T(8,128)(2,1)S(1)} %all_to_all.5.rows_ref), channel_id=1, source_target_pairs={{0,16},{16,0},{1,17},{17,1},{2,18},{18,2},{3,19},{19,3},{4,20},{20... | collective-permute-start | bytes 3538952 | tf_op jit(solution)/shard_map/ppermute | solution.py:29
  32.2 5.7 %collective-permute-start.1 = (bf16[96,1008]{1,0:T(8,128)(2,1)S(1)}, bf16[96,1008]{1,0:T(8,128)(2,1)S(1)}, u32[]{:S(2)}, u32[]{:S(2)}) collective-permute-start(bf16[96,1008]{1,0:T(8,128)(2,1)S(1)} %get-tuple-element.53), channel_id=1, source_target_pairs={{0,14},{2,0},{4,2},{6,4},{8,6},{10,8},{12,10},{14,12},{1,15},{3,1}... | collective-permute-start | bytes 580616 | tf_op jit(solution)/shard_map/ppermute | solution.py:45
  39.0 2.7 %collective-permute-start.10 = (bf16[96,1008]{1,0:T(8,128)(2,1)S(1)}, bf16[96,1008]{1,0:T(8,128)(2,1)S(1)}, u32[]{:S(2)}, u32[]{:S(2)}) collective-permute-start(bf16[96,1008]{1,0:T(8,128)(2,1)S(1)} %get-tuple-element.63), channel_id=1, source_target_pairs={{0,14},{2,0},{4,2},{6,4},{8,6},{10,8},{12,10},{14,12},{1,15},{3,1}... | collective-permute-start | bytes 580616 | tf_op jit(solution)/shard_map/ppermute | solution.py:45
  42.2 3.1 %collective-permute-done.2 = bf16[96,1008]{1,0:T(8,128)(2,1)S(1)} collective-permute-done((bf16[96,1008]{1,0:T(8,128)(2,1)S(1)}, bf16[96,1008]{1,0:T(8,128)(2,1)S(1)}, u32[]{:S(2)}, u32[]{:S(2)}) %collective-permute-start.2) | collective-permute-done | bytes 193568 | tf_op jit(solution)/shard_map/ppermute | solution.py:45
  50.5 3.0 %collective-permute-start.4 = (bf16[96,1008]{1,0:T(8,128)(2,1)S(1)}, bf16[96,1008]{1,0:T(8,128)(2,1)S(1)}, u32[]{:S(2)}, u32[]{:S(2)}) collective-permute-start(bf16[96,1008]{1,0:T(8,128)(2,1)S(1)} %add_convert_fusion.8), channel_id=1, source_target_pairs={{0,14},{2,0},{4,2},{6,4},{8,6},{10,8},{12,10},{14,12},{1,15},{3,1}... | collective-permute-start | bytes 580616 | tf_op jit(solution)/shard_map/ppermute | solution.py:45
  53.8 2.7 %collective-permute-start.11 = (bf16[96,1008]{1,0:T(8,128)(2,1)S(1)}, bf16[96,1008]{1,0:T(8,128)(2,1)S(1)}, u32[]{:S(2)}, u32[]{:S(2)}) collective-permute-start(bf16[96,1008]{1,0:T(8,128)(2,1)S(1)} %add_convert_fusion.4), channel_id=1, source_target_pairs={{0,14},{2,0},{4,2},{6,4},{8,6},{10,8},{12,10},{14,12},{1,15},{3,1}... | collective-permute-start | bytes 580616 | tf_op jit(solution)/shard_map/ppermute | solution.py:45
  56.5 3.5 %collective-permute-start.5 = (bf16[96,1008]{1,0:T(8,128)(2,1)S(1)}, bf16[96,1008]{1,0:T(8,128)(2,1)S(1)}, u32[]{:S(2)}, u32[]{:S(2)}) collective-permute-start(bf16[96,1008]{1,0:T(8,128)(2,1)S(1)} %add_convert_fusion.7), channel_id=1, source_target_pairs={{0,14},{2,0},{4,2},{6,4},{8,6},{10,8},{12,10},{14,12},{1,15},{3,1}... | collective-permute-start | bytes 580616 | tf_op jit(solution)/shard_map/ppermute | solution.py:45
  60.4 3.2 %collective-permute-start.12 = (bf16[96,1008]{1,0:T(8,128)(2,1)S(1)}, bf16[96,1008]{1,0:T(8,128)(2,1)S(1)}, u32[]{:S(2)}, u32[]{:S(2)}) collective-permute-start(bf16[96,1008]{1,0:T(8,128)(2,1)S(1)} %add_convert_fusion.3), channel_id=1, source_target_pairs={{0,14},{2,0},{4,2},{6,4},{8,6},{10,8},{12,10},{14,12},{1,15},{3,1}... | collective-permute-start | bytes 580616 | tf_op jit(solution)/shard_map/ppermute | solution.py:45
  63.6 2.3 %collective-permute-done.15 = bf16[96,1008]{1,0:T(8,128)(2,1)S(1)} collective-permute-done((bf16[96,1008]{1,0:T(8,128)(2,1)S(1)}, bf16[96,1008]{1,0:T(8,128)(2,1)S(1)}, u32[]{:S(2)}, u32[]{:S(2)}) %collective-permute-start.15) | collective-permute-done | bytes 193568 | tf_op jit(solution)/shard_map/ppermute | solution.py:45
  66.4 2.7 %collective-permute-start.9 = (bf16[96,1008]{1,0:T(8,128)(2,1)S(1)}, bf16[96,1008]{1,0:T(8,128)(2,1)S(1)}, u32[]{:S(2)}, u32[]{:S(2)}) collective-permute-start(bf16[96,1008]{1,0:T(8,128)(2,1)S(1)} %pad_maximum_fusion.1.refs_0_.refs_14_), channel_id=1, source_target_pairs={{0,14},{2,0},{4,2},{6,4},{8,6},{10,8},{12,10},{14,12},{1,15},{3,1}... | collective-permute-start | bytes 580616 | tf_op jit(solution)/shard_map/ppermute | solution.py:45
  69.1 3.2 %collective-permute-done.16 = bf16[96,1008]{1,0:T(8,128)(2,1)S(1)} collective-permute-done((bf16[96,1008]{1,0:T(8,128)(2,1)S(1)}, bf16[96,1008]{1,0:T(8,128)(2,1)S(1)}, u32[]{:S(2)}, u32[]{:S(2)}) %collective-permute-start.16) | collective-permute-done | bytes 193568 | tf_op jit(solution)/shard_map/ppermute | solution.py:45
  74.9 4.5 %collective-permute-done.22.refs_9_.refs_17_ = bf16[96,1008]{1,0:T(8,128)(2,1)S(1)} collective-permute-done((bf16[96,1008]{1,0:T(8,128)(2,1)S(1)}, bf16[96,1008]{1,0:T(8,128)(2,1)S(1)}, u32[]{:S(2)}, u32[]{:S(2)}) %collective-permute-start.22) | collective-permute-done | bytes 193568 | tf_op jit(solution)/shard_map/ppermute | solution.py:45
  80.9 3.2 %collective-permute-done.17.refs_3_.refs_11_ = bf16[96,1008]{1,0:T(8,128)(2,1)S(1)} collective-permute-done((bf16[96,1008]{1,0:T(8,128)(2,1)S(1)}, bf16[96,1008]{1,0:T(8,128)(2,1)S(1)}, u32[]{:S(2)}, u32[]{:S(2)}) %collective-permute-start.17) | collective-permute-done | bytes 193568 | tf_op jit(solution)/shard_map/ppermute | solution.py:45
  89.9 3.0 %collective-permute-done.19.refs_5_.refs_6_ = bf16[96,1008]{1,0:T(8,128)(2,1)S(1)} collective-permute-done((bf16[96,1008]{1,0:T(8,128)(2,1)S(1)}, bf16[96,1008]{1,0:T(8,128)(2,1)S(1)}, u32[]{:S(2)}, u32[]{:S(2)}) %collective-permute-start.19) | collective-permute-done | bytes 193568 | tf_op jit(solution)/shard_map/ppermute | solution.py:45
  92.9 2.7 %collective-permute-start.28 = (bf16[96,1008]{1,0:T(8,128)(2,1)S(1)}, bf16[96,1008]{1,0:T(8,128)(2,1)S(1)}, u32[]{:S(2)}, u32[]{:S(2)}) collective-permute-start(bf16[96,1008]{1,0:T(8,128)(2,1)S(1)} %collective-permute-done.26.refs_13_.refs_8_), channel_id=1, source_target_pairs={{0,14},{2,0},{4,2},{6,4},{8,6},{10,8},{12,10},{14,12},{1,15},{3,1}... | collective-permute-start | bytes 580616 | tf_op jit(solution)/shard_map/ppermute | solution.py:45
  97.2 2.4 %out_near.1 = (f32[672,768]{1,0:T(8,128)S(1)}, bf16[672,768]{1,0:T(8,128)(2,1)S(1)}) custom-call(s32[4]{0:T(128)S(1)} %pad_add_fusion.where_ref, bf16[768,384]{1,0:T(8,128)(2,1)S(1)} %maximum_maximum_fusion.w_rows_ref, bf16[368,384]{1,0:T(8,128)(2,1)S(1)} %concatenate.16.w_grads_ref, bf16[96,1008]{1,0:T(8,128)(2,1)S(1)} %pad_maximum_fusion.1.refs_0_.refs_14_, ...), custom_call_target="tpu_custom_call" | custom-call | flops 1 | bytes 1 | tf_op jit(solution)/shard_map/out_near/pallas_call | solution.py:53
  99.6 1.8 %collective-permute-done.27.refs_0_.refs_4_ = bf16[96,1008]{1,0:T(8,128)(2,1)S(1)} collective-permute-done((bf16[96,1008]{1,0:T(8,128)(2,1)S(1)}, bf16[96,1008]{1,0:T(8,128)(2,1)S(1)}, u32[]{:S(2)}, u32[]{:S(2)}) %collective-permute-start.27) | collective-permute-done | bytes 193568 | tf_op jit(solution)/shard_map/ppermute | solution.py:45
  102.4 8.3 %collective-permute-start.29 = (bf16[768,768]{1,0:T(8,128)(2,1)S(1)}, bf16[768,768]{1,0:T(8,128)(2,1)S(1)}, u32[]{:S(2)}, u32[]{:S(2)}) collective-permute-start(bf16[768,768]{1,0:T(8,128)(2,1)S(1)} %pad_maximum_fusion), channel_id=1, source_target_pairs={{0,16},{16,0},{1,17},{17,1},{2,18},{18,2},{3,19},{19,3},{4,20},{20... | collective-permute-start | bytes 3538952 | tf_op jit(solution)/shard_map/ppermute | solution.py:29
  110.7 2.8 %weight_grads.1 = (f32[192,1008]{1,0:T(8,128)S(1)}, bf16[192,1008]{1,0:T(8,128)(2,1)S(1)}) custom-call(s32[4]{0:T(128)S(1)} %pad_add_fusion.where_ref, bf16[288,768]{1,0:T(8,128)(2,1)S(1)} %get-tuple-element.75.refs_0_, bf16[288,768]{1,0:T(8,128)(2,1)S(1)} %get-tuple-element.76.refs_1_, bf16[480,768]{1,0:T(8,128)(2,1)S(1)} %get-tuple-element.77.refs_2_, ...), custom_call_target="tpu_custom_call" | custom-call | flops 1 | bytes 1 | tf_op jit(solution)/shard_map/weight_grads/pallas_call | solution.py:53
  117.7 2.6 %collective-permute-start.33 = (bf16[96,768]{1,0:T(8,128)(2,1)S(1)}, bf16[96,768]{1,0:T(8,128)(2,1)S(1)}, u32[]{:S(2)}, u32[]{:S(2)}) collective-permute-start(bf16[96,768]{1,0:T(8,128)(2,1)S(1)} %get-tuple-element.92), channel_id=1, source_target_pairs={{0,192},{64,0},{128,64},{192,128},{1,193},{65,1},{129,65},{193,129... | collective-permute-start | bytes 442376 | tf_op jit(solution)/shard_map/ppermute | solution.py:41
  120.4 4.2 %collective-permute-done.31 = bf16[2,96,768]{2,1,0:T(8,128)(2,1)S(1)} collective-permute-done((bf16[2,96,768]{2,1,0:T(8,128)(2,1)S(1)}, bf16[2,96,768]{2,1,0:T(8,128)(2,1)S(1)}, u32[]{:S(2)}, u32[]{:S(2)}) %collective-permute-start.31) | collective-permute-done | bytes 294944 | tf_op jit(solution)/shard_map/ppermute | solution.py:41
  130.8 4.3 %collective-permute-done.36.refs_4_ = bf16[96,768]{1,0:T(8,128)(2,1)S(1)} collective-permute-done((bf16[96,768]{1,0:T(8,128)(2,1)S(1)}, bf16[96,768]{1,0:T(8,128)(2,1)S(1)}, u32[]{:S(2)}, u32[]{:S(2)}) %collective-permute-start.36) | collective-permute-done | bytes 147488 | tf_op jit(solution)/shard_map/ppermute | solution.py:37
  (99 shorter events, 33.1 us)
Async XLA Ops:
  28.3 9.6 %collective-permute-start = (bf16[8,96,768]{2,1,0:T(8,128)(2,1)S(1)}, bf16[8,96,768]{2,1,0:T(8,128)(2,1)S(1)}, u32[]{:S(2)}, u32[]{:S(2)}) collective-permute-start(bf16[8,96,768]{2,1,0:T(8,128)(2,1)S(1)} %all_to_all.5.rows_ref), channel_id=1, source_target_pairs={{0,16},{16,0},{1,17},{17,1},{2,18},{18,2},{3,19},{19,3},{4,20},{20... | collective-permute-start | bytes 3538952 | tf_op jit(solution)/shard_map/ppermute | solution.py:29
  32.2 10.0 %collective-permute-start.1 = (bf16[96,1008]{1,0:T(8,128)(2,1)S(1)}, bf16[96,1008]{1,0:T(8,128)(2,1)S(1)}, u32[]{:S(2)}, u32[]{:S(2)}) collective-permute-start(bf16[96,1008]{1,0:T(8,128)(2,1)S(1)} %get-tuple-element.53), channel_id=1, source_target_pairs={{0,14},{2,0},{4,2},{6,4},{8,6},{10,8},{12,10},{14,12},{1,15},{3,1}... | collective-permute-start | bytes 580616 | tf_op jit(solution)/shard_map/ppermute | solution.py:45
  39.0 14.7 %collective-permute-start.10 = (bf16[96,1008]{1,0:T(8,128)(2,1)S(1)}, bf16[96,1008]{1,0:T(8,128)(2,1)S(1)}, u32[]{:S(2)}, u32[]{:S(2)}) collective-permute-start(bf16[96,1008]{1,0:T(8,128)(2,1)S(1)} %get-tuple-element.63), channel_id=1, source_target_pairs={{0,14},{2,0},{4,2},{6,4},{8,6},{10,8},{12,10},{14,12},{1,15},{3,1}... | collective-permute-start | bytes 580616 | tf_op jit(solution)/shard_map/ppermute | solution.py:45
  41.8 8.0 %collective-permute-start.13 = (bf16[96,1008]{1,0:T(8,128)(2,1)S(1)}, bf16[96,1008]{1,0:T(8,128)(2,1)S(1)}, u32[]{:S(2)}, u32[]{:S(2)}) collective-permute-start(bf16[96,1008]{1,0:T(8,128)(2,1)S(1)} %get-tuple-element.67), channel_id=1, source_target_pairs={{0,2},{2,4},{4,6},{6,8},{8,10},{10,12},{12,14},{14,0},{1,3},{3,5},... | collective-permute-start | bytes 580616 | tf_op jit(solution)/shard_map/ppermute | solution.py:45
  49.8 10.2 %collective-permute-start.14 = (bf16[96,1008]{1,0:T(8,128)(2,1)S(1)}, bf16[96,1008]{1,0:T(8,128)(2,1)S(1)}, u32[]{:S(2)}, u32[]{:S(2)}) collective-permute-start(bf16[96,1008]{1,0:T(8,128)(2,1)S(1)} %add_convert_fusion.2), channel_id=1, source_target_pairs={{0,2},{2,4},{4,6},{6,8},{8,10},{10,12},{12,14},{14,0},{1,3},{3,5},... | collective-permute-start | bytes 580616 | tf_op jit(solution)/shard_map/ppermute | solution.py:45
  53.6 12.4 %collective-permute-start.7 = (bf16[96,1008]{1,0:T(8,128)(2,1)S(1)}, bf16[96,1008]{1,0:T(8,128)(2,1)S(1)}, u32[]{:S(2)}, u32[]{:S(2)}) collective-permute-start(bf16[96,1008]{1,0:T(8,128)(2,1)S(1)} %add_convert_fusion.5), channel_id=1, source_target_pairs={{0,2},{2,4},{4,6},{6,8},{8,10},{10,12},{12,14},{14,0},{1,3},{3,5},... | collective-permute-start | bytes 580616 | tf_op jit(solution)/shard_map/ppermute | solution.py:45
  56.5 9.5 %collective-permute-start.5 = (bf16[96,1008]{1,0:T(8,128)(2,1)S(1)}, bf16[96,1008]{1,0:T(8,128)(2,1)S(1)}, u32[]{:S(2)}, u32[]{:S(2)}) collective-permute-start(bf16[96,1008]{1,0:T(8,128)(2,1)S(1)} %add_convert_fusion.7), channel_id=1, source_target_pairs={{0,14},{2,0},{4,2},{6,4},{8,6},{10,8},{12,10},{14,12},{1,15},{3,1}... | collective-permute-start | bytes 580616 | tf_op jit(solution)/shard_map/ppermute | solution.py:45
  60.4 8.7 %collective-permute-start.12 = (bf16[96,1008]{1,0:T(8,128)(2,1)S(1)}, bf16[96,1008]{1,0:T(8,128)(2,1)S(1)}, u32[]{:S(2)}, u32[]{:S(2)}) collective-permute-start(bf16[96,1008]{1,0:T(8,128)(2,1)S(1)} %add_convert_fusion.3), channel_id=1, source_target_pairs={{0,14},{2,0},{4,2},{6,4},{8,6},{10,8},{12,10},{14,12},{1,15},{3,1}... | collective-permute-start | bytes 580616 | tf_op jit(solution)/shard_map/ppermute | solution.py:45
  66.4 7.8 %collective-permute-start.9 = (bf16[96,1008]{1,0:T(8,128)(2,1)S(1)}, bf16[96,1008]{1,0:T(8,128)(2,1)S(1)}, u32[]{:S(2)}, u32[]{:S(2)}) collective-permute-start(bf16[96,1008]{1,0:T(8,128)(2,1)S(1)} %pad_maximum_fusion.1.refs_0_.refs_14_), channel_id=1, source_target_pairs={{0,14},{2,0},{4,2},{6,4},{8,6},{10,8},{12,10},{14,12},{1,15},{3,1}... | collective-permute-start | bytes 580616 | tf_op jit(solution)/shard_map/ppermute | solution.py:45
  72.8 7.9 %collective-permute-start.21 = (bf16[96,1008]{1,0:T(8,128)(2,1)S(1)}, bf16[96,1008]{1,0:T(8,128)(2,1)S(1)}, u32[]{:S(2)}, u32[]{:S(2)}) collective-permute-start(bf16[96,1008]{1,0:T(8,128)(2,1)S(1)} %pad_maximum_fusion.2.refs_7_.refs_19_), channel_id=1, source_target_pairs={{0,2},{2,4},{4,6},{6,8},{8,10},{10,12},{12,14},{14,0},{1,3},{3,5},... | collective-permute-start | bytes 580616 | tf_op jit(solution)/shard_map/ppermute | solution.py:45
  74.9 9.2 %collective-permute-start.17 = (bf16[96,1008]{1,0:T(8,128)(2,1)S(1)}, bf16[96,1008]{1,0:T(8,128)(2,1)S(1)}, u32[]{:S(2)}, u32[]{:S(2)}) collective-permute-start(bf16[96,1008]{1,0:T(8,128)(2,1)S(1)} %collective-permute-done.8.refs_1_.refs_13_), channel_id=1, source_target_pairs={{0,2},{2,4},{4,6},{6,8},{8,10},{10,12},{12,14},{14,0},{1,3},{3,5},... | collective-permute-start | bytes 580616 | tf_op jit(solution)/shard_map/ppermute | solution.py:45
  79.4 9.0 %collective-permute-start.18 = (bf16[96,1008]{1,0:T(8,128)(2,1)S(1)}, bf16[96,1008]{1,0:T(8,128)(2,1)S(1)}, u32[]{:S(2)}, u32[]{:S(2)}) collective-permute-start(bf16[96,1008]{1,0:T(8,128)(2,1)S(1)} %collective-permute-done.9.refs_2_.refs_12_), channel_id=1, source_target_pairs={{0,14},{2,0},{4,2},{6,4},{8,6},{10,8},{12,10},{14,12},{1,15},{3,1}... | collective-permute-start | bytes 580616 | tf_op jit(solution)/shard_map/ppermute | solution.py:45
  80.6 8.7 %collective-permute-start.23 = (bf16[96,1008]{1,0:T(8,128)(2,1)S(1)}, bf16[96,1008]{1,0:T(8,128)(2,1)S(1)}, u32[]{:S(2)}, u32[]{:S(2)}) collective-permute-start(bf16[96,1008]{1,0:T(8,128)(2,1)S(1)} %collective-permute-done.21.refs_8_.refs_18_), channel_id=1, source_target_pairs={{0,2},{2,4},{4,6},{6,8},{8,10},{10,12},{12,14},{14,0},{1,3},{3,5},... | collective-permute-start | bytes 580616 | tf_op jit(solution)/shard_map/ppermute | solution.py:45
  84.1 8.8 %collective-permute-start.19 = (bf16[96,1008]{1,0:T(8,128)(2,1)S(1)}, bf16[96,1008]{1,0:T(8,128)(2,1)S(1)}, u32[]{:S(2)}, u32[]{:S(2)}) collective-permute-start(bf16[96,1008]{1,0:T(8,128)(2,1)S(1)} %collective-permute-done.17.refs_3_.refs_11_), channel_id=1, source_target_pairs={{0,2},{2,4},{4,6},{6,8},{8,10},{10,12},{12,14},{14,0},{1,3},{3,5},... | collective-permute-start | bytes 580616 | tf_op jit(solution)/shard_map/ppermute | solution.py:45
  85.0 7.9 %collective-permute-start.26 = (bf16[96,1008]{1,0:T(8,128)(2,1)S(1)}, bf16[96,1008]{1,0:T(8,128)(2,1)S(1)}, u32[]{:S(2)}, u32[]{:S(2)}) collective-permute-start(bf16[96,1008]{1,0:T(8,128)(2,1)S(1)} %collective-permute-done.24.refs_11_.refs_15_), channel_id=1, source_target_pairs={{0,14},{2,0},{4,2},{6,4},{8,6},{10,8},{12,10},{14,12},{1,15},{3,1}... | collective-permute-start | bytes 580616 | tf_op jit(solution)/shard_map/ppermute | solution.py:45
  89.3 7.8 %collective-permute-start.25 = (bf16[96,1008]{1,0:T(8,128)(2,1)S(1)}, bf16[96,1008]{1,0:T(8,128)(2,1)S(1)}, u32[]{:S(2)}, u32[]{:S(2)}) collective-permute-start(bf16[96,1008]{1,0:T(8,128)(2,1)S(1)} %collective-permute-done.23.refs_10_.refs_16_), channel_id=1, source_target_pairs={{0,2},{2,4},{4,6},{6,8},{8,10},{10,12},{12,14},{14,0},{1,3},{3,5},... | collective-permute-start | bytes 580616 | tf_op jit(solution)/shard_map/ppermute | solution.py:45
  92.9 8.5 %collective-permute-start.27 = (bf16[96,1008]{1,0:T(8,128)(2,1)S(1)}, bf16[96,1008]{1,0:T(8,128)(2,1)S(1)}, u32[]{:S(2)}, u32[]{:S(2)}) collective-permute-start(bf16[96,1008]{1,0:T(8,128)(2,1)S(1)} %collective-permute-done.19.refs_5_.refs_6_), channel_id=1, source_target_pairs={{0,2},{2,4},{4,6},{6,8},{8,10},{10,12},{12,14},{14,0},{1,3},{3,5},... | collective-permute-start | bytes 580616 | tf_op jit(solution)/shard_map/ppermute | solution.py:45
  92.9 8.5 %collective-permute-start.28 = (bf16[96,1008]{1,0:T(8,128)(2,1)S(1)}, bf16[96,1008]{1,0:T(8,128)(2,1)S(1)}, u32[]{:S(2)}, u32[]{:S(2)}) collective-permute-start(bf16[96,1008]{1,0:T(8,128)(2,1)S(1)} %collective-permute-done.26.refs_13_.refs_8_), channel_id=1, source_target_pairs={{0,14},{2,0},{4,2},{6,4},{8,6},{10,8},{12,10},{14,12},{1,15},{3,1}... | collective-permute-start | bytes 580616 | tf_op jit(solution)/shard_map/ppermute | solution.py:45
  102.4 11.1 %collective-permute-start.29 = (bf16[768,768]{1,0:T(8,128)(2,1)S(1)}, bf16[768,768]{1,0:T(8,128)(2,1)S(1)}, u32[]{:S(2)}, u32[]{:S(2)}) collective-permute-start(bf16[768,768]{1,0:T(8,128)(2,1)S(1)} %pad_maximum_fusion), channel_id=1, source_target_pairs={{0,16},{16,0},{1,17},{17,1},{2,18},{18,2},{3,19},{19,3},{4,20},{20... | collective-permute-start | bytes 3538952 | tf_op jit(solution)/shard_map/ppermute | solution.py:29
  114.4 10.2 %collective-permute-start.31 = (bf16[2,96,768]{2,1,0:T(8,128)(2,1)S(1)}, bf16[2,96,768]{2,1,0:T(8,128)(2,1)S(1)}, u32[]{:S(2)}, u32[]{:S(2)}) collective-permute-start(bf16[2,96,768]{2,1,0:T(8,128)(2,1)S(1)} %slice_bitcast_fusion), channel_id=1, source_target_pairs={{0,128},{64,192},{128,0},{192,64},{1,129},{65,193},{129,1},{193,65... | collective-permute-start | bytes 884744 | tf_op jit(solution)/shard_map/ppermute | solution.py:41
  115.7 13.9 %collective-permute-start.30 = (bf16[192,1008]{1,0:T(8,128)(2,1)S(1)}, bf16[192,1008]{1,0:T(8,128)(2,1)S(1)}, u32[]{:S(2)}, u32[]{:S(2)}) collective-permute-start(bf16[192,1008]{1,0:T(8,128)(2,1)S(1)} %get-tuple-element.82), channel_id=1, source_target_pairs={{0,1},{1,0},{2,3},{3,2},{4,5},{5,4},{6,7},{7,6},{8,9},{9,8},{10,11... | collective-permute-start | bytes 1161224 | tf_op jit(solution)/shard_map/ppermute | solution.py:327
  116.2 10.1 %collective-permute-start.35 = (bf16[96,768]{1,0:T(8,128)(2,1)S(1)}, bf16[96,768]{1,0:T(8,128)(2,1)S(1)}, u32[]{:S(2)}, u32[]{:S(2)}) collective-permute-start(bf16[96,768]{1,0:T(8,128)(2,1)S(1)} %get-tuple-element.89), channel_id=1, source_target_pairs={{0,192},{64,0},{128,64},{192,128},{1,193},{65,1},{129,65},{193,129... | collective-permute-start | bytes 442376 | tf_op jit(solution)/shard_map/ppermute | solution.py:41
  117.7 10.3 %collective-permute-start.34 = (bf16[96,768]{1,0:T(8,128)(2,1)S(1)}, bf16[96,768]{1,0:T(8,128)(2,1)S(1)}, u32[]{:S(2)}, u32[]{:S(2)}) collective-permute-start(bf16[96,768]{1,0:T(8,128)(2,1)S(1)} %get-tuple-element.90), channel_id=1, source_target_pairs={{0,64},{64,128},{128,192},{192,0},{1,65},{65,129},{129,193},{193,1... | collective-permute-start | bytes 442376 | tf_op jit(solution)/shard_map/ppermute | solution.py:41
  117.7 13.1 %collective-permute-start.33 = (bf16[96,768]{1,0:T(8,128)(2,1)S(1)}, bf16[96,768]{1,0:T(8,128)(2,1)S(1)}, u32[]{:S(2)}, u32[]{:S(2)}) collective-permute-start(bf16[96,768]{1,0:T(8,128)(2,1)S(1)} %get-tuple-element.92), channel_id=1, source_target_pairs={{0,192},{64,0},{128,64},{192,128},{1,193},{65,1},{129,65},{193,129... | collective-permute-start | bytes 442376 | tf_op jit(solution)/shard_map/ppermute | solution.py:41
  (18 other events, 174.4 us)
